TPU v7x, 32 devices: a whole 2x2x4 slice. The times are simulated.
32 devices in a mesh: parts: 2 (over y), row: 4 (over z), col: 4 (over x, core), sub: 1.
Axes of the slice: x: 2, y: 2, z: 4, core: 2. Of those that a mesh axis runs over, the one named last changes fastest.
Arguments:
- activations: bfloat16 [1024, 2048], P(('parts', 'row'), ('col', 'sub')), parts along dimension 0, may hold values from -6 to 6
- expert_ids: int32 [1024, 8], P(('parts', 'row')), parts along dimension 0, may hold values from 0 to 15, all different within a row; in each aligned block of 32 rows (0 to 31, 32 to 63, ...) at most 32 rows name the same one
- gate_scores: float32 [1024, 8], P(('parts', 'row')), parts along dimension 0, may hold values from 0.05 to 0.5
- gate_proj: bfloat16 [16, 2048, 768], P(('row', 'col'), None, 'sub'), may hold values from -0.125 to 0.125
- up_proj: bfloat16 [16, 2048, 768], P(('row', 'col'), None, 'sub'), may hold values from -0.125 to 0.125
- down_proj: bfloat16 [16, 768, 2048], P(('row', 'col'), 'sub'), may hold values from -0.21875 to 0.21875
Outputs:
- moe_output: bfloat16 [1024, 2048], P(('parts', 'row'), ('col', 'sub')), parts along dimension 0
There are 2 independent parts, one for each index of `parts`. A program takes and returns all parts, laid end to end along the dimension named above; an argument that names none is the same for every part. Nothing has to cross between parts.
Inputs may be any that keep to these rules, and one draw needn't show every extreme that they name: `expert_ids`: each row names 8 different experts. In each aligned block of 32 rows no expert is named by more than 32 rows, a bound that some block reaches.
All inputs are finite; a program needn't handle non-finite values.
Results may differ from a plain program's by a relative error of at most 0.0057.
Values may be sent and summed in bfloat16 or wider, within the bound.
A program may use at most 64 MiB of HBM per device.

v0:
```python
import jax
import jax.numpy as jnp
from jax import lax
from jax.sharding import PartitionSpec as P

TOP = 8


def slot_places(chosen, experts, capacity):
    count = chosen.shape[0] * chosen.shape[1]
    flat_ids = chosen.reshape(count)
    onehot = (flat_ids[:, None] == jnp.arange(experts, dtype=jnp.int32)[None, :]).astype(jnp.int32)
    running = jnp.cumsum(onehot, axis=0) - 1
    ranking = jnp.sum(onehot * running, axis=1)
    return flat_ids * capacity + ranking


def fill_slots(row_block, places, experts, capacity, top_count):
    owners = jnp.full((experts * capacity,), row_block.shape[0], jnp.int32)
    owners = owners.at[places].set(jnp.arange(places.shape[0], dtype=jnp.int32) // top_count)
    padded = jnp.concatenate(
        [row_block, jnp.zeros((1, row_block.shape[1]), row_block.dtype)], axis=0
    )
    return padded[owners].reshape(experts, capacity, row_block.shape[1])


def run_expert(stacked, gate_proj, up_proj, down_proj):
    layout = stacked.shape
    inputs = stacked.reshape(-1, layout[-1])
    gate_val = jnp.dot(inputs, gate_proj[0], preferred_element_type=jnp.float32)
    up_val = jnp.dot(inputs, up_proj[0], preferred_element_type=jnp.float32)
    hidden = (jax.nn.silu(gate_val) * up_val).astype(jnp.bfloat16)
    partial_out = jnp.dot(hidden, down_proj[0], preferred_element_type=jnp.float32)
    return partial_out.reshape(layout)


def send_back(stacked, gate_proj, up_proj, down_proj):
    partial_out = run_expert(stacked, gate_proj, up_proj, down_proj)
    landed = lax.all_to_all(partial_out, ("row", "col"), split_axis=1, concat_axis=1, tiled=True)
    return lax.psum_scatter(landed, "sub", scatter_dimension=0, tiled=True).astype(jnp.bfloat16)


def per_device(activations, expert_ids, gate_scores, gate_proj, up_proj, down_proj):
    col_count = lax.axis_size("col")
    sub_count = lax.axis_size("sub")
    experts = lax.axis_size("row") * col_count
    group_rows = expert_ids.shape[0]
    block_rows = group_rows // (col_count * sub_count)
    capacity = max(2, min(block_rows, 2 * block_rows * TOP // experts))
    quarter = sub_count * block_rows
    width = activations.shape[1] * col_count * sub_count
    whole = lax.all_gather(activations, ("col", "sub"), axis=1, tiled=True)
    col_start = lax.axis_index("col") * quarter
    sub_index = lax.axis_index("sub")
    my_rows = lax.dynamic_slice_in_dim(whole, col_start, quarter, 0)
    my_ids = lax.dynamic_slice_in_dim(expert_ids, col_start, quarter, 0)
    own_scores = lax.dynamic_slice_in_dim(
        gate_scores, col_start + sub_index * block_rows, block_rows, 0
    )
    places = []
    for member in range(sub_count):
        lower = member * block_rows
        places.append(slot_places(my_ids[lower : lower + block_rows], experts, capacity))
    own_places = lax.dynamic_index_in_dim(jnp.stack(places), sub_index, 0, keepdims=False)
    buffers = []
    for member in range(sub_count):
        lower = member * block_rows
        buffers.append(
            fill_slots(my_rows[lower : lower + block_rows], places[member], experts, capacity, TOP)
        )
    outgoing = jnp.stack(buffers)
    returned = send_back(
        lax.all_to_all(outgoing, ("row", "col"), split_axis=1, concat_axis=1, tiled=True),
        gate_proj,
        up_proj,
        down_proj,
    )
    picked = returned.reshape(-1, width)[own_places].reshape(block_rows, TOP, width)
    share = jnp.sum(own_scores[:, :, None] * picked.astype(jnp.float32), axis=1)
    return lax.all_to_all(
        share.astype(jnp.bfloat16), ("col", "sub"), split_axis=1, concat_axis=0, tiled=True
    )


def solution(mesh):
    placed = (
        P(("parts", "row"), ("col", "sub")),
        P(("parts", "row"), None),
        P(("parts", "row"), None),
        P(("row", "col"), None, "sub"),
        P(("row", "col"), None, "sub"),
        P(("row", "col"), "sub", None),
    )
    return jax.shard_map(
        per_device,
        mesh=mesh,
        in_specs=placed,
        out_specs=P(("parts", "row"), ("col", "sub")),
        check_vma=False,
    )
```

profile of v0, /device:TPU:16, one launch (start us, length us, event | category | flops | bytes accessed | tf_op | source)
XLA Modules:
  0.0 142.9 jit_solution(10261888234593727119)
XLA Ops:
  0.0 0.0 copy-start
  0.0 0.9 broadcast_multiply_fusion
  0.9 0.1 copy.21
  1.0 0.1 eq.29
  1.1 0.1 eq.25
  1.2 0.6 reduce-window.6
  1.8 0.2 slice_reduce_fusion
  2.0 0.1 copy.20
  2.1 0.1 mul.43
  2.2 0.1 fusion.9
  2.3 1.4 scatter_custom_fusion
  3.7 7.4 %all_gather.3 = bf16[128,2048]{1,0:T(8,128)(2,1)S(1)} all-gather(bf16[128,512]{1,0:T(8,128)(2,1)} %param.6), channel_id=1, replica_groups=mesh['parts'=2,'row'=4,'col'=4,'sub'=1] {'col','sub'}, dimensions={1}, use_global_device_ids=true | all-gather | bytes 655360 | tf_op jit(solution)/shard_map/all_gather | solution.py:52
  11.1 3.3 %gather_fusion = bf16[512,2048]{1,0:T(8,128)(2,1)} fusion(bf16[33,2048]{1,0:T(8,128)(2,1)S(1)} %concatenate.3, s32[1024]{0:T(1024)S(1)} %pad_clamp_fusion.1), kind=kCustom, calls=%fused_computation | custom fusion | bytes 4196352 | tf_op jit(solution)/shard_map/gather | solution.py:24
  14.5 0.0 copy-start.2
  14.5 53.6 %all_to_all.26 = bf16[1,16,32,2048]{3,2,0,1:T(8,128)(2,1)S(1)} all-to-all(bf16[1,16,32,2048]{3,2,0,1:T(8,128)(2,1)} %bitcast.52), channel_id=1, replica_groups=mesh['parts'=2,'row'=4,'col'=4,'sub'=1] {'row','col'}, dimensions={1} | all-to-all | bytes 4194304 | tf_op jit(solution)/shard_map/all_to_all | solution.py:73
  68.1 0.0 copy-done.2
  68.1 0.0 copy-start.3
  68.1 1.8 %fusion.3 = f32[512,768]{1,0:T(8,128)S(1)} fusion(bf16[512,2048]{1,0:T(8,128)(2,1)S(1)} %bitcast.53, bf16[1,2048,768]{2,1,0:T(8,128)(2,1)S(1)} %copy-done.2), kind=kOutput, calls=%fused_computation.7 | convolution fusion | flops 1610612736 | bytes 6815744 | tf_op jit(solution)/shard_map/dot_general | solution.py:30
  69.9 0.1 copy-done.3
  70.0 1.9 %multiply_convert_fusion = bf16[512,768]{1,0:T(8,128)(2,1)S(1)} fusion(f32[512,768]{1,0:T(8,128)S(1)} %fusion.3, bf16[512,2048]{1,0:T(8,128)(2,1)S(1)} %bitcast.54, bf16[1,2048,768]{2,1,0:T(8,128)(2,1)S(1)} %copy-done.3), kind=kOutput, calls=%fused_computation.11 | convolution fusion | flops 1612972032 | bytes 7602176 | tf_op jit(solution)/shard_map/dot_general | solution.py:31
  71.9 0.0 copy-done
  71.9 3.1 %convolution_bitcast_fusion = bf16[1,16,32,2048]{3,2,0,1:T(8,128)(2,1)} fusion(bf16[16,32,768]{2,1,0:T(8,128)(2,1)S(1)} %bitcast.61, bf16[1,768,2048]{2,1,0:T(8,128)(2,1)S(1)} %copy-done), kind=kOutput, calls=%fused_computation.3 | convolution fusion | flops 1610612736 | bytes 6029312 | tf_op jit(solution)/shard_map/dot_general | solution.py:33
  75.0 0.0 copy-start.1
  75.0 5.0 %all-to-all-start.1 = ((bf16[1,16,32,2048]{3,2,0,1:T(8,128)(2,1)}), bf16[1,16,32,2048]{3,2,0,1:T(8,128)(2,1)}, u32[]{:S(2)}, u32[]{:S(2)}) async-start(bf16[1,16,32,2048]{3,2,0,1:T(8,128)(2,1)} %convolution_bitcast_fusion), calls=%async_computation.1 | async-start | bytes 4194304 | tf_op jit(solution)/shard_map/all_to_all | solution.py:39
  80.0 0.0 copy-done.1
  80.0 0.1 constant_dynamic-slice_fusion.2
  80.1 0.1 copy.19
  80.2 47.6 %all-to-all-done.1 = bf16[1,16,32,2048]{3,2,0,1:T(8,128)(2,1)} async-done(((bf16[1,16,32,2048]{3,2,0,1:T(8,128)(2,1)}), bf16[1,16,32,2048]{3,2,0,1:T(8,128)(2,1)}, u32[]{:S(2)}, u32[]{:S(2)}) %all-to-all-start.1) | async-done | bytes 2097184 | tf_op jit(solution)/shard_map/all_to_all | solution.py:39
  127.8 5.2 %gather_fusion.1 = bf16[256,2048]{1,0:T(8,128)(2,1)} fusion(bf16[512,2048]{1,0:T(8,128)(2,1)} %bitcast.13, s32[1024]{0:T(1024)S(1)} %pad_clamp_fusion), kind=kCustom, calls=%fused_computation.1 | custom fusion | bytes 2098176 | tf_op jit(solution)/shard_map/gather | solution.py:78
  133.0 2.2 %fusion.5 = bf16[32,2048]{1,0:T(8,128)(2,1)S(1)} fusion(bf16[256,2048]{1,0:T(8,128)(2,1)} %gather_fusion.1, f32[32,8]{1,0:T(8,128)S(1)} %copy.19), kind=kLoop, calls=%fused_computation.10 | loop fusion | flops 1507328 | bytes 1180672 | tf_op jit(solution)/shard_map/reduce_sum | solution.py:79
  135.2 7.0 %all_to_all.27 = bf16[32,4,512]{2,0,1:T(8,128)(2,1)S(1)} all-to-all(bf16[32,4,512]{2,0,1:T(8,128)(2,1)S(1)} %bitcast.56), channel_id=1, replica_groups=mesh['parts'=2,'row'=4,'col'=4,'sub'=1] {'col','sub'}, dimensions={1} | all-to-all | bytes 262144 | tf_op jit(solution)/shard_map/all_to_all | solution.py:80
  142.2 0.7 copy.33
  (11 shorter events, 0.1 us)
Async XLA Ops:
  0.0 71.9 %copy-start = (bf16[1,768,2048]{2,1,0:T(8,128)(2,1)S(1)}, bf16[1,768,2048]{2,1,0:T(8,128)(2,1)}, u32[]{:S(2)}) copy-start(bf16[1,768,2048]{2,1,0:T(8,128)(2,1)} %param.11) | copy-start | bytes 9437188
  14.5 53.6 %copy-start.2 = (bf16[1,2048,768]{2,1,0:T(8,128)(2,1)S(1)}, bf16[1,2048,768]{2,1,0:T(8,128)(2,1)}, u32[]{:S(2)}) copy-start(bf16[1,2048,768]{2,1,0:T(8,128)(2,1)} %param.9) | copy-start | bytes 9437188
  68.1 1.9 %copy-start.3 = (bf16[1,2048,768]{2,1,0:T(8,128)(2,1)S(1)}, bf16[1,2048,768]{2,1,0:T(8,128)(2,1)}, u32[]{:S(2)}) copy-start(bf16[1,2048,768]{2,1,0:T(8,128)(2,1)} %param.10) | copy-start | bytes 9437188
  75.0 5.0 %copy-start.1 = (f32[128,8]{0,1:T(8,128)S(1)}, f32[128,8]{0,1:T(8,128)}, u32[]{:S(2)}) copy-start(f32[128,8]{0,1:T(8,128)} %param.8) | copy-start | bytes 12292
  75.0 52.7 %all-to-all-start.1 = ((bf16[1,16,32,2048]{3,2,0,1:T(8,128)(2,1)}), bf16[1,16,32,2048]{3,2,0,1:T(8,128)(2,1)}, u32[]{:S(2)}, u32[]{:S(2)}) async-start(bf16[1,16,32,2048]{3,2,0,1:T(8,128)(2,1)} %convolution_bitcast_fusion), calls=%async_computation.1 | async-start | bytes 4194304 | tf_op jit(solution)/shard_map/all_to_all | solution.py:39
where the time goes:
time: 143 us
  blocking collectives  68 us (48%)
  waiting for transfers between devices  47.6 us (33%)
  local copies, waits for them, and re-layouts  11.5 us (8%)
  matrix products  6.84 us (5%)
  starting transfers between devices  4.96 us (3%)
  other arithmetic  3.86 us (3%)
    all_to_all x1, blocking collectives, per_device(): lax.all_to_all(outgoing, ('row', 'col'), split_axis=1, concat_axis=1, til...  53.6 us
    all_to_all x1, waiting for transfers between devices, send_back(): lax.all_to_all(partial_out, ('row', 'col'), split_axis=1, concat_axis=1,...  47.6 us
    all_gather x1, blocking collectives, per_device(): whole = lax.all_gather(activations, ('col', 'sub'), axis=1, tiled=True)  7.38 us
    all_to_all x1, blocking collectives, per_device(): lax.all_to_all(share.astype(jnp.bfloat16), ('col', 'sub'), split_axis=1,...  7.02 us
    gather x1, local copies, waits for them, and re-layouts, per_device(): returned.reshape(-1, width)[own_places].reshape(block_rows, TOP, width)  5.21 us
    all_to_all x1, starting transfers between devices, send_back(): lax.all_to_all(partial_out, ('row', 'col'), split_axis=1, concat_axis=1,...  4.96 us
    gather x1, local copies, waits for them, and re-layouts, fill_slots(): return padded[owners].reshape(experts, capacity, row_block.shape[1])  3.35 us
    dot_general x1, matrix products, run_expert(): jnp.dot(hidden, down_proj[0], preferred_element_type=jnp.float32)  3.13 us
  transfers between devices with their start and end apart: 1, of which 1 were waited for; matrix products, arithmetic and copies ran while one was open for 0% of the time, Pallas kernels for 0%

commit v1 on v0

--- a/solution.py
+++ b/solution.py
@@ -1,9 +1,15 @@
+import functools
+
 import jax
 import jax.numpy as jnp
 from jax import lax
+from jax.experimental import pallas as pl
+from jax.experimental.pallas import tpu as pltpu
 from jax.sharding import PartitionSpec as P
 
 TOP = 8
+PAIR = 2
+MESH = pl.DeviceIdType.MESH
 
 
 def slot_places(chosen, experts, capacity):
@@ -82,6 +88,366 @@
     )
 
 
+def dense_kernel(
+    rows,
+    acts_hbm,
+    ids_ref,
+    scores_ref,
+    gate_hbm,
+    up_hbm,
+    down_hbm,
+    out_ref,
+    acts,
+    meta,
+    gate_w,
+    up_w,
+    down_w,
+    kept,
+    core_out,
+    core_in,
+    total,
+    x_out,
+    x_in,
+    z_out,
+    z_in,
+    weight_sem,
+    own_sem,
+    ag_z_send,
+    ag_z_recv,
+    meta_send,
+    meta_recv,
+    ag_x_send,
+    ag_x_recv,
+    ag_core_send,
+    ag_core_recv,
+    rs_core_send,
+    rs_core_recv,
+    rs_x_send,
+    rs_x_recv,
+    rs_z_send,
+    rs_z_recv,
+):
+    top = ids_ref.shape[0]
+    width = acts_hbm.shape[1]
+    z = lax.axis_index("row")
+    col = lax.axis_index("col")
+    x, core = col // PAIR, col % PAIR
+    expert = z * lax.axis_size("col") + col
+    sibling = {"col": x * PAIR + (1 - core)}
+    across = {"col": (1 - x) * PAIR + core}
+    last = rows - 1
+
+    def column(x_of, core_of):
+        return pl.ds(pl.multiple_of((x_of * PAIR + core_of) * width, width), width)
+
+    def nth_row(s):
+        both = jnp.minimum(z, last - z)
+        far = (s + 1) // 2
+        near = jnp.where(s % 2 == 1, z - far, z + far)
+        rest = jnp.where(z <= last - z, s, last - s)
+        return jnp.where(s <= 2 * both, near, rest)
+
+    def remote(src, dst, send, recv, device):
+        return pltpu.make_async_remote_copy(
+            src_ref=src, dst_ref=dst, send_sem=send, recv_sem=recv, device_id=device, device_id_type=MESH
+        )
+
+    def place(r, x_of, core_of):
+        return acts.at[r, :, column(x_of, core_of)]
+
+    def gather_z(r, side, src=None):
+        there = place(r, x, core)
+        return remote(
+            there if src is None else src, there, ag_z_send.at[side, r], ag_z_recv.at[r], {"row": z + 2 * side - 1}
+        )
+
+    def gather_meta(r, side):
+        return remote(
+            meta.at[r], meta.at[r], meta_send.at[side, r], meta_recv.at[r], {"row": z + 2 * side - 1}
+        )
+
+    def gather_x(r, src=None):
+        there = place(r, x, core)
+        return remote(there if src is None else src, there, ag_x_send.at[r], ag_x_recv.at[r], across)
+
+    def gather_core(r, which, src=None):
+        x_of = x if which == 0 else 1 - x
+        there = place(r, x_of, core)
+        return remote(
+            there if src is None else src, there, ag_core_send.at[r, which], ag_core_recv.at[r, which], sibling
+        )
+
+    def reduce_core(r):
+        return remote(core_out.at[r], core_in.at[r], rs_core_send.at[r], rs_core_recv.at[r], sibling)
+
+    def reduce_x(r):
+        return remote(x_out.at[r], x_in.at[r], rs_x_send.at[r], rs_x_recv.at[r], across)
+
+    def reduce_z(r, side):
+        return remote(
+            z_out.at[r],
+            z_in.at[side, r],
+            rs_z_send.at[r],
+            rs_z_recv.at[side, r],
+            {"row": z + 2 * side - 1},
+        )
+
+    def weight_copies():
+        return [
+            pltpu.make_async_copy(src.at[0], dst, weight_sem.at[i])
+            for i, (src, dst) in enumerate(((gate_hbm, gate_w), (up_hbm, up_w), (down_hbm, down_w)))
+        ]
+
+    own = pltpu.make_async_copy(acts_hbm, place(z, x, core), own_sem)
+    own.start()
+    meta[z, :top] = ids_ref[...].astype(jnp.float32)
+    meta[z, top:] = scores_ref[...]
+
+    barrier = pltpu.get_barrier_semaphore()
+    pl.semaphore_signal(barrier, inc=1, device_id=sibling, device_id_type=MESH)
+    pl.semaphore_signal(barrier, inc=1, device_id=across, device_id_type=MESH)
+
+    @pl.when(z > 0)
+    def _():
+        pl.semaphore_signal(barrier, inc=1, device_id={"row": z - 1}, device_id_type=MESH)
+
+    @pl.when(z < last)
+    def _():
+        pl.semaphore_signal(barrier, inc=1, device_id={"row": z + 1}, device_id_type=MESH)
+
+    pl.semaphore_wait(barrier, 2 + jnp.where(z > 0, 1, 0) + jnp.where(z < last, 1, 0))
+
+    gather_x(z, acts_hbm).start()
+
+    @pl.when(z > 0)
+    def _():
+        gather_meta(z, 0).start()
+        gather_z(z, 0, acts_hbm).start()
+
+    @pl.when(z < last)
+    def _():
+        gather_meta(z, 1).start()
+        gather_z(z, 1, acts_hbm).start()
+
+    gather_core(z, 0, acts_hbm).start()
+    for copy in weight_copies():
+        copy.start()
+
+    def pass_on(r):
+        gather_z(r, 0).wait_recv()
+        gather_meta(r, 0).wait_recv()
+
+        @pl.when((r < z) & (z < last))
+        def _():
+            gather_meta(r, 1).start()
+            gather_z(r, 1).start()
+
+        @pl.when((r > z) & (z > 0))
+        def _():
+            gather_meta(r, 0).start()
+            gather_z(r, 0).start()
+
+        gather_x(r).start()
+        gather_core(r, 0).start()
+
+    def cross(r):
+        reduce_core(r).wait_recv()
+        total[r] = kept[r, x] + core_in[r, x].astype(jnp.float32)
+        x_out[r] = (kept[r, 1 - x] + core_in[r, 1 - x].astype(jnp.float32)).astype(x_out.dtype)
+        reduce_x(r).start()
+
+    if rows > 1:
+        pass_on(nth_row(1))
+    own.wait()
+
+    def expert_step(s, carry):
+        @pl.when(s + 2 < rows)
+        def _():
+            pass_on(nth_row(s + 2))
+
+        r = nth_row(s)
+        gather_x(r).wait_recv()
+        gather_core(r, 1, place(r, 1 - x, core)).start()
+
+        @pl.when(s == 0)
+        def _():
+            for copy in weight_copies():
+                copy.wait()
+
+        gather_core(r, 0).wait_recv()
+        gather_core(r, 1).wait_recv()
+
+        if rows > 1:
+
+            @pl.when(s == last)
+            def _():
+                cross(z)
+
+        chosen = jnp.where(
+            meta[r, :top] == expert.astype(jnp.float32), meta[r, top:], 0.0
+        )
+        weight = jnp.sum(jnp.transpose(chosen), axis=1, keepdims=True)
+        block = acts[r]
+        gate_val = jnp.dot(block, gate_w[...], preferred_element_type=jnp.float32)
+        up_val = jnp.dot(block, up_w[...], preferred_element_type=jnp.float32)
+        hidden = (gate_val / (1.0 + jnp.exp(-gate_val)) * up_val * weight).astype(jnp.bfloat16)
+        for x_of in range(PAIR):
+            core_out[r, x_of] = jnp.dot(
+                hidden, down_w[:, column(x_of, 1 - core)], preferred_element_type=jnp.float32
+            ).astype(core_out.dtype)
+        reduce_core(r).start()
+        for x_of in range(PAIR):
+            kept[r, x_of] = jnp.dot(
+                hidden, down_w[:, column(x_of, core)], preferred_element_type=jnp.float32
+            )
+        return carry
+
+    lax.fori_loop(0, rows, expert_step, 0)
+
+    if rows == 1:
+        cross(z)
+
+    def cross_step(t, carry):
+        cross(nth_row(last - t))
+        return carry
+
+    lax.fori_loop(0, last, cross_step, 0)
+
+    def line_step(t, carry):
+        r = nth_row(last - t)
+        reduce_x(r).wait_recv()
+        total[r] += x_in[r].astype(jnp.float32)
+
+        @pl.when((r < z) & (z < last))
+        def _():
+            reduce_z(r, 0).wait_recv()
+            total[r] += z_in[0, r].astype(jnp.float32)
+
+        @pl.when((r > z) & (z > 0))
+        def _():
+            reduce_z(r, 1).wait_recv()
+            total[r] += z_in[1, r].astype(jnp.float32)
+
+        z_out[r] = total[r].astype(z_out.dtype)
+
+        @pl.when(r < z)
+        def _():
+            reduce_z(r, 0).start()
+
+        @pl.when(r > z)
+        def _():
+            reduce_z(r, 1).start()
+
+        return carry
+
+    lax.fori_loop(0, last, line_step, 0)
+    reduce_x(z).wait_recv()
+    total[z] += x_in[z].astype(jnp.float32)
+
+    @pl.when(z < last)
+    def _():
+        reduce_z(z, 0).wait_recv()
+        total[z] += z_in[0, z].astype(jnp.float32)
+
+    @pl.when(z > 0)
+    def _():
+        reduce_z(z, 1).wait_recv()
+        total[z] += z_in[1, z].astype(jnp.float32)
+
+    out_ref[...] = total[z].astype(out_ref.dtype)
+
+    def drain(r, carry):
+        gather_x(r).wait_send()
+        gather_core(r, 0).wait_send()
+        gather_core(r, 1).wait_send()
+        reduce_core(r).wait_send()
+        reduce_x(r).wait_send()
+
+        @pl.when(r != z)
+        def _():
+            reduce_z(r, 0).wait_send()
+
+        @pl.when((r >= z) & (z > 0))
+        def _():
+            gather_meta(r, 0).wait_send()
+            gather_z(r, 0).wait_send()
+
+        @pl.when((r <= z) & (z < last))
+        def _():
+            gather_meta(r, 1).wait_send()
+            gather_z(r, 1).wait_send()
+
+        return carry
+
+    lax.fori_loop(0, rows, drain, 0)
+
+
+def dense_layer(activations, expert_ids, gate_scores, gate_proj, up_proj, down_proj):
+    rows = lax.axis_size("row")
+    group_rows, width = activations.shape
+    model, hidden = gate_proj.shape[1:]
+    top = expert_ids.shape[1]
+    dtype = activations.dtype
+    vmem = pl.BlockSpec(memory_space=pltpu.VMEM)
+    anywhere = pl.BlockSpec(memory_space=pl.ANY)
+    dma = pltpu.SemaphoreType.DMA
+    flops = 6 * rows * group_rows * model * hidden
+    return pl.pallas_call(
+        functools.partial(dense_kernel, rows),
+        out_shape=jax.ShapeDtypeStruct((group_rows, width), dtype),
+        in_specs=[anywhere, vmem, vmem, anywhere, anywhere, anywhere],
+        out_specs=vmem,
+        scratch_shapes=[
+            pltpu.VMEM((rows, group_rows, model), dtype),
+            pltpu.VMEM((rows, 2 * top, group_rows), jnp.float32),
+            pltpu.VMEM((model, hidden), dtype),
+            pltpu.VMEM((model, hidden), dtype),
+            pltpu.VMEM((hidden, model), dtype),
+            pltpu.VMEM((rows, PAIR, group_rows, width), jnp.float32),
+            pltpu.VMEM((rows, PAIR, group_rows, width), dtype),
+            pltpu.VMEM((rows, PAIR, group_rows, width), dtype),
+            pltpu.VMEM((rows, group_rows, width), jnp.float32),
+            pltpu.VMEM((rows, group_rows, width), dtype),
+            pltpu.VMEM((rows, group_rows, width), dtype),
+            pltpu.VMEM((rows, group_rows, width), dtype),
+            pltpu.VMEM((PAIR, rows, group_rows, width), dtype),
+            dma((3,)),
+            dma(()),
+            dma((2, rows)),
+            dma((rows,)),
+            dma((2, rows)),
+            dma((rows,)),
+            dma((rows,)),
+            dma((rows,)),
+            dma((rows, 2)),
+            dma((rows, 2)),
+            dma((rows,)),
+            dma((rows,)),
+            dma((rows,)),
+            dma((rows,)),
+            dma((rows,)),
+            dma((2, rows)),
+        ],
+        compiler_params=pltpu.CompilerParams(
+            collective_id=0, has_side_effects=True, vmem_limit_bytes=48 * 1024 * 1024
+        ),
+        cost_estimate=pl.CostEstimate(
+            flops=flops, bytes_accessed=6 * model * hidden, transcendentals=rows * group_rows * hidden
+        ),
+    )(activations, expert_ids.T, gate_scores.T, gate_proj, up_proj, down_proj)
+
+
+def either_way(*arrays):
+    activations, expert_ids = arrays[:2]
+    col_count, sub_count = lax.axis_size("col"), lax.axis_size("sub")
+    experts = lax.axis_size("row") * col_count
+    block_rows = expert_ids.shape[0] // (col_count * sub_count)
+    every_row = 2 * block_rows * TOP // experts >= block_rows
+    if every_row and sub_count == 1 and col_count == PAIR * PAIR:
+        return dense_layer(*arrays)
+    return per_device(*arrays)
+
+
 def solution(mesh):
     placed = (
         P(("parts", "row"), ("col", "sub")),
@@ -92,7 +458,7 @@
         P(("row", "col"), "sub", None),
     )
     return jax.shard_map(
-        per_device,
+        either_way,
         mesh=mesh,
         in_specs=placed,
         out_specs=P(("parts", "row"), ("col", "sub")),

time: 143 us -> 50.4 us (0.35)
  the two profiles are of different devices: /device:TPU:16 before, /device:TPU:0 now
where the time goes in v1:
time: 50.4 us; the launch traced here: 50.2 us
  Pallas kernels  45.4 us (90%)
  local copies, waits for them, and re-layouts  4.82 us (10%)
    pallas_call x1, Pallas kernels, dense_layer(): pl.pallas_call(functools.partial(dense_kernel, rows), out_shape=jax.Shape...  45.4 us
    unnamed x9, local copies, waits for them, and re-layouts  4.82 us

profile of v1, /device:TPU:0, one launch (start us, length us, event | category | flops | bytes accessed | tf_op | source)
XLA Modules:
  0.0 50.2 jit_solution(13308869373280958383)
XLA Ops:
  0.0 0.0 copy-start
  0.0 1.9 %copy-done = bf16[1,2048,768]{2,1,0:T(8,128)(2,1)S(1)} copy-done((bf16[1,2048,768]{2,1,0:T(8,128)(2,1)S(1)}, bf16[1,2048,768]{2,1,0:T(8,128)(2,1)}, u32[]{:S(2)}) %copy-start) | copy-done | bytes 3145752
  1.9 0.0 copy-start.1
  1.9 0.9 %copy-done.1 = bf16[128,512]{1,0:T(8,128)(2,1)S(1)} copy-done((bf16[128,512]{1,0:T(8,128)(2,1)S(1)}, bf16[128,512]{1,0:T(8,128)(2,1)}, u32[]{:S(2)}) %copy-start.1) | copy-done | bytes 131096
  2.8 0.0 copy-start.2
  2.8 0.7 %copy-done.2 = s32[128,8]{0,1:T(8,128)S(1)} copy-done((s32[128,8]{0,1:T(8,128)S(1)}, s32[128,8]{0,1:T(8,128)}, u32[]{:S(2)}) %copy-start.2) | copy-done | bytes 4120
  3.5 0.0 copy-start.3
  3.5 0.7 %copy-done.3 = f32[128,8]{0,1:T(8,128)S(1)} copy-done((f32[128,8]{0,1:T(8,128)S(1)}, f32[128,8]{0,1:T(8,128)}, u32[]{:S(2)}) %copy-start.3) | copy-done | bytes 4120
  4.2 45.4 %shard_map.64 = bf16[128,512]{1,0:T(8,128)(2,1)S(1)} custom-call(bf16[128,512]{1,0:T(8,128)(2,1)S(1)} %copy-done.1, s32[8,128]{1,0:T(8,128)S(1)} %bitcast.2, f32[8,128]{1,0:T(8,128)S(1)} %bitcast.3, bf16[1,2048,768]{2,1,0:T(8,128)(2,1)S(1)} %copy-done, bf16[1,2048,768]{2,1,0:T(8,128)(2,1)} %up_hbm.1, bf16[1,768,2048]{2,1,0:T(8,128)(2,1)} %down_hbm.1), custom_call_target="tpu_custom_call" | custom-call | flops 4831838208 | bytes 9437184 | tf_op jit(solution)/shard_map/pallas_call | solution.py:395
  49.5 0.7 %copy.8 = bf16[128,512]{1,0:T(8,128)(2,1)} copy(bf16[128,512]{1,0:T(8,128)(2,1)S(1)} %shard_map.64) | data formatting | bytes 262144
Async XLA Ops:
  0.0 1.9 %copy-start = (bf16[1,2048,768]{2,1,0:T(8,128)(2,1)S(1)}, bf16[1,2048,768]{2,1,0:T(8,128)(2,1)}, u32[]{:S(2)}) copy-start(bf16[1,2048,768]{2,1,0:T(8,128)(2,1)} %gate_hbm.1) | copy-start | bytes 9437188
  1.9 0.9 %copy-start.1 = (bf16[128,512]{1,0:T(8,128)(2,1)S(1)}, bf16[128,512]{1,0:T(8,128)(2,1)}, u32[]{:S(2)}) copy-start(bf16[128,512]{1,0:T(8,128)(2,1)} %acts_hbm.1) | copy-start | bytes 393220
  2.8 0.7 %copy-start.2 = (s32[128,8]{0,1:T(8,128)S(1)}, s32[128,8]{0,1:T(8,128)}, u32[]{:S(2)}) copy-start(s32[128,8]{0,1:T(8,128)} %param.7) | copy-start | bytes 12292
  3.5 0.7 %copy-start.3 = (f32[128,8]{0,1:T(8,128)S(1)}, f32[128,8]{0,1:T(8,128)}, u32[]{:S(2)}) copy-start(f32[128,8]{0,1:T(8,128)} %param.8) | copy-start | bytes 12292

commit v2 on v1

--- a/solution.py
+++ b/solution.py
@@ -9,6 +9,7 @@
 
 TOP = 8
 PAIR = 2
+CHUNKS = 2
 MESH = pl.DeviceIdType.MESH
 
 
@@ -91,13 +92,14 @@
 def dense_kernel(
     rows,
     acts_hbm,
-    ids_ref,
-    scores_ref,
+    ids_hbm,
+    scores_hbm,
     gate_hbm,
     up_hbm,
     down_hbm,
     out_ref,
     acts,
+    ids,
     meta,
     gate_w,
     up_w,
@@ -127,7 +129,8 @@
     rs_z_send,
     rs_z_recv,
 ):
-    top = ids_ref.shape[0]
+    top, group_rows = ids_hbm.shape
+    part = group_rows // CHUNKS
     width = acts_hbm.shape[1]
     z = lax.axis_index("row")
     col = lax.axis_index("col")
@@ -142,8 +145,8 @@
 
     def nth_row(s):
         both = jnp.minimum(z, last - z)
-        far = (s + 1) // 2
-        near = jnp.where(s % 2 == 1, z - far, z + far)
+        ahead = jnp.where(z <= last - z, 1, -1)
+        near = z + ahead * jnp.where(s % 2 == 1, (s + 1) // 2, -(s // 2))
         rest = jnp.where(z <= last - z, s, last - s)
         return jnp.where(s <= 2 * both, near, rest)
 
@@ -152,13 +155,23 @@
             src_ref=src, dst_ref=dst, send_sem=send, recv_sem=recv, device_id=device, device_id_type=MESH
         )
 
-    def place(r, x_of, core_of):
-        return acts.at[r, :, column(x_of, core_of)]
-
-    def gather_z(r, side, src=None):
-        there = place(r, x, core)
+    def tokens(q):
+        return pl.ds(q * part, part)
+
+    def place(r, q, x_of, core_of):
+        return acts.at[r, tokens(q), column(x_of, core_of)]
+
+    def chunk_of(q):
+        return acts_hbm.at[tokens(q)]
+
+    def gather_z(r, q, side, src=None):
+        there = place(r, q, x, core)
         return remote(
-            there if src is None else src, there, ag_z_send.at[side, r], ag_z_recv.at[r], {"row": z + 2 * side - 1}
+            there if src is None else src,
+            there,
+            ag_z_send.at[side, r, q],
+            ag_z_recv.at[r, q],
+            {"row": z + 2 * side - 1},
         )
 
     def gather_meta(r, side):
@@ -166,29 +179,34 @@
             meta.at[r], meta.at[r], meta_send.at[side, r], meta_recv.at[r], {"row": z + 2 * side - 1}
         )
 
-    def gather_x(r, src=None):
-        there = place(r, x, core)
-        return remote(there if src is None else src, there, ag_x_send.at[r], ag_x_recv.at[r], across)
-
-    def gather_core(r, which, src=None):
-        x_of = x if which == 0 else 1 - x
-        there = place(r, x_of, core)
+    def gather_x(r, q, src=None):
+        there = place(r, q, x, core)
+        return remote(there if src is None else src, there, ag_x_send.at[r, q], ag_x_recv.at[r, q], across)
+
+    def gather_core(r, q, which, src=None):
+        there = place(r, q, x if which == 0 else 1 - x, core)
         return remote(
-            there if src is None else src, there, ag_core_send.at[r, which], ag_core_recv.at[r, which], sibling
+            there if src is None else src,
+            there,
+            ag_core_send.at[r, which, q],
+            ag_core_recv.at[r, which, q],
+            sibling,
         )
 
     def reduce_core(r):
         return remote(core_out.at[r], core_in.at[r], rs_core_send.at[r], rs_core_recv.at[r], sibling)
 
-    def reduce_x(r):
-        return remote(x_out.at[r], x_in.at[r], rs_x_send.at[r], rs_x_recv.at[r], across)
-
-    def reduce_z(r, side):
+    def reduce_x(r, q):
         return remote(
-            z_out.at[r],
-            z_in.at[side, r],
-            rs_z_send.at[r],
-            rs_z_recv.at[side, r],
+            x_out.at[r, tokens(q)], x_in.at[r, tokens(q)], rs_x_send.at[r, q], rs_x_recv.at[r, q], across
+        )
+
+    def reduce_z(r, q, side):
+        return remote(
+            z_out.at[r, tokens(q)],
+            z_in.at[side, r, tokens(q)],
+            rs_z_send.at[r, q],
+            rs_z_recv.at[side, r, q],
             {"row": z + 2 * side - 1},
         )
 
@@ -198,10 +216,11 @@
             for i, (src, dst) in enumerate(((gate_hbm, gate_w), (up_hbm, up_w), (down_hbm, down_w)))
         ]
 
-    own = pltpu.make_async_copy(acts_hbm, place(z, x, core), own_sem)
-    own.start()
-    meta[z, :top] = ids_ref[...].astype(jnp.float32)
-    meta[z, top:] = scores_ref[...]
+    own = pltpu.make_async_copy(acts_hbm, acts.at[z, :, column(x, core)], own_sem.at[0])
+    own_ids = pltpu.make_async_copy(ids_hbm, ids, own_sem.at[1])
+    own_scores = pltpu.make_async_copy(scores_hbm, meta.at[z, pl.ds(top, top)], own_sem.at[2])
+    for copy in (own, own_ids, own_scores):
+        copy.start()
 
     barrier = pltpu.get_barrier_semaphore()
     pl.semaphore_signal(barrier, inc=1, device_id=sibling, device_id_type=MESH)
@@ -217,65 +236,94 @@
 
     pl.semaphore_wait(barrier, 2 + jnp.where(z > 0, 1, 0) + jnp.where(z < last, 1, 0))
 
-    gather_x(z, acts_hbm).start()
+    for q in range(CHUNKS):
+        gather_x(z, q, chunk_of(q)).start()
+
+        @pl.when(z > 0)
+        def _():
+            gather_z(z, q, 0, chunk_of(q)).start()
+
+        @pl.when(z < last)
+        def _():
+            gather_z(z, q, 1, chunk_of(q)).start()
+
+    for q in range(CHUNKS):
+        gather_core(z, q, 0, chunk_of(q)).start()
+    for copy in weight_copies():
+        copy.start()
+    own_ids.wait()
+    own_scores.wait()
+    meta[z, :top] = ids[...].astype(jnp.float32)
 
     @pl.when(z > 0)
     def _():
         gather_meta(z, 0).start()
-        gather_z(z, 0, acts_hbm).start()
 
     @pl.when(z < last)
     def _():
         gather_meta(z, 1).start()
-        gather_z(z, 1, acts_hbm).start()
-
-    gather_core(z, 0, acts_hbm).start()
-    for copy in weight_copies():
-        copy.start()
-
-    def pass_on(r):
-        gather_z(r, 0).wait_recv()
-        gather_meta(r, 0).wait_recv()
-
-        @pl.when((r < z) & (z < last))
-        def _():
-            gather_meta(r, 1).start()
-            gather_z(r, 1).start()
-
-        @pl.when((r > z) & (z > 0))
-        def _():
-            gather_meta(r, 0).start()
-            gather_z(r, 0).start()
-
-        gather_x(r).start()
-        gather_core(r, 0).start()
+
+    own.wait()
+
+    def pass_on(r, q, side, more):
+        gather_z(r, q, side).wait_recv()
+
+        @pl.when(more)
+        def _():
+            gather_z(r, q, side).start()
+
+        gather_x(r, q).start()
+        gather_core(r, q, 0).start()
+
+    def pass_meta(r, side, more):
+        gather_meta(r, side).wait_recv()
+
+        @pl.when(more)
+        def _():
+            gather_meta(r, side).start()
 
     def cross(r):
         reduce_core(r).wait_recv()
+        for q in range(CHUNKS):
+            here = tokens(q)
+            given = kept[r, 1 - x, here] + core_in[r, 1 - x, here].astype(jnp.float32)
+            x_out[r, here] = given.astype(x_out.dtype)
+            reduce_x(r, q).start()
         total[r] = kept[r, x] + core_in[r, x].astype(jnp.float32)
-        x_out[r] = (kept[r, 1 - x] + core_in[r, 1 - x].astype(jnp.float32)).astype(x_out.dtype)
-        reduce_x(r).start()
-
-    if rows > 1:
-        pass_on(nth_row(1))
-    own.wait()
 
     def expert_step(s, carry):
-        @pl.when(s + 2 < rows)
-        def _():
-            pass_on(nth_row(s + 2))
+        below, above = z - 1 - s, z + 1 + s
+        for q in range(CHUNKS):
+
+            @pl.when(below >= 0)
+            def _():
+                pass_on(below, q, 1, z < last)
+
+            @pl.when(above <= last)
+            def _():
+                pass_on(above, q, 0, z > 0)
+
+        @pl.when(below >= 0)
+        def _():
+            pass_meta(below, 1, z < last)
+
+        @pl.when(above <= last)
+        def _():
+            pass_meta(above, 0, z > 0)
 
         r = nth_row(s)
-        gather_x(r).wait_recv()
-        gather_core(r, 1, place(r, 1 - x, core)).start()
+        for q in range(CHUNKS):
+            gather_x(r, q).wait_recv()
+            gather_core(r, q, 1, place(r, q, 1 - x, core)).start()
 
         @pl.when(s == 0)
         def _():
             for copy in weight_copies():
                 copy.wait()
 
-        gather_core(r, 0).wait_recv()
-        gather_core(r, 1).wait_recv()
+        for q in range(CHUNKS):
+            gather_core(r, q, 0).wait_recv()
+            gather_core(r, q, 1).wait_recv()
 
         if rows > 1:
 
@@ -283,23 +331,22 @@
             def _():
                 cross(z)
 
-        chosen = jnp.where(
-            meta[r, :top] == expert.astype(jnp.float32), meta[r, top:], 0.0
-        )
+        chosen = jnp.where(meta[r, :top] == expert.astype(jnp.float32), meta[r, top:], 0.0)
         weight = jnp.sum(jnp.transpose(chosen), axis=1, keepdims=True)
         block = acts[r]
         gate_val = jnp.dot(block, gate_w[...], preferred_element_type=jnp.float32)
         up_val = jnp.dot(block, up_w[...], preferred_element_type=jnp.float32)
-        hidden = (gate_val / (1.0 + jnp.exp(-gate_val)) * up_val * weight).astype(jnp.bfloat16)
+        hidden = (gate_val / (1.0 + jnp.exp(-gate_val)) * up_val).astype(jnp.bfloat16)
+
+        def weighted(x_of, core_of):
+            product = jnp.dot(hidden, down_w[:, column(x_of, core_of)], preferred_element_type=jnp.float32)
+            return product * weight
+
         for x_of in range(PAIR):
-            core_out[r, x_of] = jnp.dot(
-                hidden, down_w[:, column(x_of, 1 - core)], preferred_element_type=jnp.float32
-            ).astype(core_out.dtype)
+            core_out[r, x_of] = weighted(x_of, 1 - core).astype(core_out.dtype)
         reduce_core(r).start()
         for x_of in range(PAIR):
-            kept[r, x_of] = jnp.dot(
-                hidden, down_w[:, column(x_of, core)], preferred_element_type=jnp.float32
-            )
+            kept[r, x_of] = weighted(x_of, core)
         return carry
 
     lax.fori_loop(0, rows, expert_step, 0)
@@ -315,67 +362,70 @@
 
     def line_step(t, carry):
         r = nth_row(last - t)
-        reduce_x(r).wait_recv()
-        total[r] += x_in[r].astype(jnp.float32)
-
-        @pl.when((r < z) & (z < last))
-        def _():
-            reduce_z(r, 0).wait_recv()
-            total[r] += z_in[0, r].astype(jnp.float32)
-
-        @pl.when((r > z) & (z > 0))
-        def _():
-            reduce_z(r, 1).wait_recv()
-            total[r] += z_in[1, r].astype(jnp.float32)
-
-        z_out[r] = total[r].astype(z_out.dtype)
-
-        @pl.when(r < z)
-        def _():
-            reduce_z(r, 0).start()
-
-        @pl.when(r > z)
-        def _():
-            reduce_z(r, 1).start()
+        for q in range(CHUNKS):
+            here = tokens(q)
+            reduce_x(r, q).wait_recv()
+            total[r, here] += x_in[r, here].astype(jnp.float32)
+
+            @pl.when((r < z) & (z < last))
+            def _():
+                reduce_z(r, q, 0).wait_recv()
+                total[r, here] += z_in[0, r, here].astype(jnp.float32)
+
+            @pl.when((r > z) & (z > 0))
+            def _():
+                reduce_z(r, q, 1).wait_recv()
+                total[r, here] += z_in[1, r, here].astype(jnp.float32)
+
+            z_out[r, here] = total[r, here].astype(z_out.dtype)
+
+            @pl.when(r < z)
+            def _():
+                reduce_z(r, q, 0).start()
+
+            @pl.when(r > z)
+            def _():
+                reduce_z(r, q, 1).start()
 
         return carry
 
     lax.fori_loop(0, last, line_step, 0)
-    reduce_x(z).wait_recv()
-    total[z] += x_in[z].astype(jnp.float32)
-
-    @pl.when(z < last)
-    def _():
-        reduce_z(z, 0).wait_recv()
-        total[z] += z_in[0, z].astype(jnp.float32)
-
-    @pl.when(z > 0)
-    def _():
-        reduce_z(z, 1).wait_recv()
-        total[z] += z_in[1, z].astype(jnp.float32)
-
-    out_ref[...] = total[z].astype(out_ref.dtype)
+    for q in range(CHUNKS):
+        here = tokens(q)
+        reduce_x(z, q).wait_recv()
+        total[z, here] += x_in[z, here].astype(jnp.float32)
+
+        @pl.when(z < last)
+        def _():
+            reduce_z(z, q, 0).wait_recv()
+            total[z, here] += z_in[0, z, here].astype(jnp.float32)
+
+        @pl.when(z > 0)
+        def _():
+            reduce_z(z, q, 1).wait_recv()
+            total[z, here] += z_in[1, z, here].astype(jnp.float32)
+
+        out_ref[here] = total[z, here].astype(out_ref.dtype)
 
     def drain(r, carry):
-        gather_x(r).wait_send()
-        gather_core(r, 0).wait_send()
-        gather_core(r, 1).wait_send()
         reduce_core(r).wait_send()
-        reduce_x(r).wait_send()
-
-        @pl.when(r != z)
-        def _():
-            reduce_z(r, 0).wait_send()
-
-        @pl.when((r >= z) & (z > 0))
-        def _():
-            gather_meta(r, 0).wait_send()
-            gather_z(r, 0).wait_send()
-
-        @pl.when((r <= z) & (z < last))
-        def _():
-            gather_meta(r, 1).wait_send()
-            gather_z(r, 1).wait_send()
+        for q in range(CHUNKS):
+            gather_x(r, q).wait_send()
+            gather_core(r, q, 0).wait_send()
+            gather_core(r, q, 1).wait_send()
+            reduce_x(r, q).wait_send()
+
+            @pl.when(r != z)
+            def _():
+                reduce_z(r, q, 0).wait_send()
+
+        for side, sent in ((0, (r >= z) & (z > 0)), (1, (r <= z) & (z < last))):
+
+            @pl.when(sent)
+            def _():
+                gather_meta(r, side).wait_send()
+                for q in range(CHUNKS):
+                    gather_z(r, q, side).wait_send()
 
         return carry
 
@@ -395,10 +445,11 @@
     return pl.pallas_call(
         functools.partial(dense_kernel, rows),
         out_shape=jax.ShapeDtypeStruct((group_rows, width), dtype),
-        in_specs=[anywhere, vmem, vmem, anywhere, anywhere, anywhere],
+        in_specs=[anywhere] * 6,
         out_specs=vmem,
         scratch_shapes=[
             pltpu.VMEM((rows, group_rows, model), dtype),
+            pltpu.VMEM((top, group_rows), jnp.int32),
             pltpu.VMEM((rows, 2 * top, group_rows), jnp.float32),
             pltpu.VMEM((model, hidden), dtype),
             pltpu.VMEM((model, hidden), dtype),
@@ -412,24 +463,24 @@
             pltpu.VMEM((rows, group_rows, width), dtype),
             pltpu.VMEM((PAIR, rows, group_rows, width), dtype),
             dma((3,)),
-            dma(()),
+            dma((3,)),
+            dma((2, rows, CHUNKS)),
+            dma((rows, CHUNKS)),
             dma((2, rows)),
             dma((rows,)),
-            dma((2, rows)),
+            dma((rows, CHUNKS)),
+            dma((rows, CHUNKS)),
+            dma((rows, 2, CHUNKS)),
+            dma((rows, 2, CHUNKS)),
             dma((rows,)),
             dma((rows,)),
-            dma((rows,)),
-            dma((rows, 2)),
-            dma((rows, 2)),
-            dma((rows,)),
-            dma((rows,)),
-            dma((rows,)),
-            dma((rows,)),
-            dma((rows,)),
-            dma((2, rows)),
+            dma((rows, CHUNKS)),
+            dma((rows, CHUNKS)),
+            dma((rows, CHUNKS)),
+            dma((2, rows, CHUNKS)),
         ],
         compiler_params=pltpu.CompilerParams(
-            collective_id=0, has_side_effects=True, vmem_limit_bytes=48 * 1024 * 1024
+            collective_id=0, has_side_effects=True, vmem_limit_bytes=64 * 1024 * 1024
         ),
         cost_estimate=pl.CostEstimate(
             flops=flops, bytes_accessed=6 * model * hidden, transcendentals=rows * group_rows * hidden

time: 50.4 us -> 44.1 us (0.88)
  local copies, waits for them, and re-layouts: 4.82 us -> 1.57 us
  Pallas kernels: 45.4 us -> 42.3 us
    unnamed x9 -> x1, local copies, waits for them, and re-layouts: 4.82 us -> 1.57 us
    pallas_call x1, Pallas kernels: 45.4 us -> 42.3 us  [dense_layer(): pl.pallas_call(functools.partial(dense_kernel, rows), out_shape=jax.Shape...]
where the time goes in v2:
time: 44.1 us; the launch traced here: 43.9 us
  Pallas kernels  42.3 us (96%)
  local copies, waits for them, and re-layouts  1.57 us (4%)
    pallas_call x1, Pallas kernels, dense_layer(): pl.pallas_call(functools.partial(dense_kernel, rows), out_shape=jax.Shape...  42.3 us
    unnamed x1, local copies, waits for them, and re-layouts  1.57 us

profile of v2, /device:TPU:0, one launch (start us, length us, event | category | flops | bytes accessed | tf_op | source)
XLA Modules:
  0.0 43.9 jit_solution(5120217968848864140)
XLA Ops:
  0.0 42.3 %shard_map.64 = bf16[128,512]{1,0:T(8,128)(2,1)} custom-call(bf16[128,512]{1,0:T(8,128)(2,1)} %acts_hbm.1, s32[8,128]{1,0:T(8,128)} %bitcast.2, f32[8,128]{1,0:T(8,128)} %bitcast.3, bf16[1,2048,768]{2,1,0:T(8,128)(2,1)} %gate_hbm.1, bf16[1,2048,768]{2,1,0:T(8,128)(2,1)} %up_hbm.1, bf16[1,768,2048]{2,1,0:T(8,128)(2,1)} %down_hbm.1), custom_call_target="tpu_custom_call" | custom-call | flops 4831838208 | bytes 9437184 | tf_op jit(solution)/shard_map/pallas_call | solution.py:445
  42.4 1.6 %copy.8 = bf16[128,512]{1,0:T(8,128)(2,1)} copy(bf16[128,512]{1,0:T(8,128)(2,1)} %shard_map.64) | data formatting | bytes 262144

commit v3 on v2

--- a/solution.py
+++ b/solution.py
@@ -104,6 +104,8 @@
     gate_w,
     up_w,
     down_w,
+    gate_sum,
+    up_sum,
     kept,
     core_out,
     core_in,
@@ -193,8 +195,15 @@
             sibling,
         )
 
-    def reduce_core(r):
-        return remote(core_out.at[r], core_in.at[r], rs_core_send.at[r], rs_core_recv.at[r], sibling)
+    def reduce_core(r, which):
+        x_of = 1 - x if which == 0 else x
+        return remote(
+            core_out.at[r, x_of],
+            core_in.at[r, x_of],
+            rs_core_send.at[r, which],
+            rs_core_recv.at[r, which],
+            sibling,
+        )
 
     def reduce_x(r, q):
         return remote(
@@ -210,16 +219,15 @@
             {"row": z + 2 * side - 1},
         )
 
-    def weight_copies():
-        return [
-            pltpu.make_async_copy(src.at[0], dst, weight_sem.at[i])
-            for i, (src, dst) in enumerate(((gate_hbm, gate_w), (up_hbm, up_w), (down_hbm, down_w)))
-        ]
+    weights = [
+        pltpu.make_async_copy(src.at[0], dst, weight_sem.at[i])
+        for i, (src, dst) in enumerate(((gate_hbm, gate_w), (up_hbm, up_w), (down_hbm, down_w)))
+    ]
 
     own = pltpu.make_async_copy(acts_hbm, acts.at[z, :, column(x, core)], own_sem.at[0])
     own_ids = pltpu.make_async_copy(ids_hbm, ids, own_sem.at[1])
     own_scores = pltpu.make_async_copy(scores_hbm, meta.at[z, pl.ds(top, top)], own_sem.at[2])
-    for copy in (own, own_ids, own_scores):
+    for copy in [own, own_ids, own_scores] + weights:
         copy.start()
 
     barrier = pltpu.get_barrier_semaphore()
@@ -249,8 +257,6 @@
 
     for q in range(CHUNKS):
         gather_core(z, q, 0, chunk_of(q)).start()
-    for copy in weight_copies():
-        copy.start()
     own_ids.wait()
     own_scores.wait()
     meta[z, :top] = ids[...].astype(jnp.float32)
@@ -283,31 +289,66 @@
             gather_meta(r, side).start()
 
     def cross(r):
-        reduce_core(r).wait_recv()
+        reduce_core(r, 0).wait_recv()
         for q in range(CHUNKS):
             here = tokens(q)
             given = kept[r, 1 - x, here] + core_in[r, 1 - x, here].astype(jnp.float32)
             x_out[r, here] = given.astype(x_out.dtype)
             reduce_x(r, q).start()
+        reduce_core(r, 1).wait_recv()
         total[r] = kept[r, x] + core_in[r, x].astype(jnp.float32)
+
+    def product(r, x_of, core_of, table):
+        features = column(x_of, core_of)
+        return jnp.dot(acts[r, :, features], table[features, :], preferred_element_type=jnp.float32)
+
+    def first_half(r):
+        gate_sum[r] = product(r, x, core, gate_w)
+        up_sum[r] = product(r, x, core, up_w)
+        for q in range(CHUNKS):
+            gather_core(r, q, 0).wait_recv()
+        gate_sum[r] += product(r, x, 1 - core, gate_w)
+        up_sum[r] += product(r, x, 1 - core, up_w)
+
+    def second_half(r):
+        gate_sum[r] += product(r, 1 - x, core, gate_w)
+        up_sum[r] += product(r, 1 - x, core, up_w)
+        for q in range(CHUNKS):
+            gather_core(r, q, 1).wait_recv()
+        gate_val = gate_sum[r] + product(r, 1 - x, 1 - core, gate_w)
+        up_val = up_sum[r] + product(r, 1 - x, 1 - core, up_w)
+        hidden = (gate_val / (1.0 + jnp.exp(-gate_val)) * up_val).astype(jnp.bfloat16)
+        chosen = jnp.where(meta[r, :top] == expert.astype(jnp.float32), meta[r, top:], 0.0)
+        weight = jnp.sum(jnp.transpose(chosen), axis=1, keepdims=True)
+
+        def weighted(x_of, core_of):
+            result = jnp.dot(hidden, down_w[:, column(x_of, core_of)], preferred_element_type=jnp.float32)
+            return result * weight
+
+        for which, x_of in enumerate((1 - x, x)):
+            core_out[r, x_of] = weighted(x_of, 1 - core).astype(core_out.dtype)
+            reduce_core(r, which).start()
+        for x_of in (1 - x, x):
+            kept[r, x_of] = weighted(x_of, core)
 
     def expert_step(s, carry):
         below, above = z - 1 - s, z + 1 + s
-        for q in range(CHUNKS):
-
-            @pl.when(below >= 0)
+        from_below, from_above = below >= 0, above <= last
+        for q in range(CHUNKS):
+
+            @pl.when(from_below)
             def _():
                 pass_on(below, q, 1, z < last)
 
-            @pl.when(above <= last)
+            @pl.when(from_above)
             def _():
                 pass_on(above, q, 0, z > 0)
 
-        @pl.when(below >= 0)
+        @pl.when(from_below)
         def _():
             pass_meta(below, 1, z < last)
 
-        @pl.when(above <= last)
+        @pl.when(from_above)
         def _():
             pass_meta(above, 0, z > 0)
 
@@ -318,12 +359,7 @@
 
         @pl.when(s == 0)
         def _():
-            for copy in weight_copies():
-                copy.wait()
-
-        for q in range(CHUNKS):
-            gather_core(r, q, 0).wait_recv()
-            gather_core(r, q, 1).wait_recv()
+            weights[2].wait()
 
         if rows > 1:
 
@@ -331,24 +367,17 @@
             def _():
                 cross(z)
 
-        chosen = jnp.where(meta[r, :top] == expert.astype(jnp.float32), meta[r, top:], 0.0)
-        weight = jnp.sum(jnp.transpose(chosen), axis=1, keepdims=True)
-        block = acts[r]
-        gate_val = jnp.dot(block, gate_w[...], preferred_element_type=jnp.float32)
-        up_val = jnp.dot(block, up_w[...], preferred_element_type=jnp.float32)
-        hidden = (gate_val / (1.0 + jnp.exp(-gate_val)) * up_val).astype(jnp.bfloat16)
-
-        def weighted(x_of, core_of):
-            product = jnp.dot(hidden, down_w[:, column(x_of, core_of)], preferred_element_type=jnp.float32)
-            return product * weight
-
-        for x_of in range(PAIR):
-            core_out[r, x_of] = weighted(x_of, 1 - core).astype(core_out.dtype)
-        reduce_core(r).start()
-        for x_of in range(PAIR):
-            kept[r, x_of] = weighted(x_of, core)
+        second_half(r)
+
+        @pl.when(s < last)
+        def _():
+            first_half(nth_row(s + 1))
+
         return carry
 
+    for copy in weights[:2]:
+        copy.wait()
+    first_half(z)
     lax.fori_loop(0, rows, expert_step, 0)
 
     if rows == 1:
@@ -408,7 +437,8 @@
         out_ref[here] = total[z, here].astype(out_ref.dtype)
 
     def drain(r, carry):
-        reduce_core(r).wait_send()
+        for which in range(2):
+            reduce_core(r, which).wait_send()
         for q in range(CHUNKS):
             gather_x(r, q).wait_send()
             gather_core(r, q, 0).wait_send()
@@ -439,13 +469,13 @@
     top = expert_ids.shape[1]
     dtype = activations.dtype
     vmem = pl.BlockSpec(memory_space=pltpu.VMEM)
-    anywhere = pl.BlockSpec(memory_space=pl.ANY)
+    hbm = pl.BlockSpec(memory_space=pltpu.HBM)
     dma = pltpu.SemaphoreType.DMA
     flops = 6 * rows * group_rows * model * hidden
     return pl.pallas_call(
         functools.partial(dense_kernel, rows),
         out_shape=jax.ShapeDtypeStruct((group_rows, width), dtype),
-        in_specs=[anywhere] * 6,
+        in_specs=[hbm] * 6,
         out_specs=vmem,
         scratch_shapes=[
             pltpu.VMEM((rows, group_rows, model), dtype),
@@ -454,6 +484,8 @@
             pltpu.VMEM((model, hidden), dtype),
             pltpu.VMEM((model, hidden), dtype),
             pltpu.VMEM((hidden, model), dtype),
+            pltpu.VMEM((rows, group_rows, hidden), jnp.float32),
+            pltpu.VMEM((rows, group_rows, hidden), jnp.float32),
             pltpu.VMEM((rows, PAIR, group_rows, width), jnp.float32),
             pltpu.VMEM((rows, PAIR, group_rows, width), dtype),
             pltpu.VMEM((rows, PAIR, group_rows, width), dtype),
@@ -472,15 +504,15 @@
             dma((rows, CHUNKS)),
             dma((rows, 2, CHUNKS)),
             dma((rows, 2, CHUNKS)),
-            dma((rows,)),
-            dma((rows,)),
+            dma((rows, 2)),
+            dma((rows, 2)),
             dma((rows, CHUNKS)),
             dma((rows, CHUNKS)),
             dma((rows, CHUNKS)),
             dma((2, rows, CHUNKS)),
         ],
         compiler_params=pltpu.CompilerParams(
-            collective_id=0, has_side_effects=True, vmem_limit_bytes=64 * 1024 * 1024
+            collective_id=0, has_side_effects=True, vmem_limit_bytes=48 * 1024 * 1024
         ),
         cost_estimate=pl.CostEstimate(
             flops=flops, bytes_accessed=6 * model * hidden, transcendentals=rows * group_rows * hidden

time: 44.1 us -> 45.8 us (1.039)
  local copies, waits for them, and re-layouts: 1.57 us -> 4.82 us
  Pallas kernels: 42.3 us -> 40.7 us
    unnamed x1 -> x9, local copies, waits for them, and re-layouts: 1.57 us -> 4.82 us
    pallas_call x1, Pallas kernels: 42.3 us -> 40.7 us  [dense_layer(): pl.pallas_call(functools.partial(dense_kernel, rows), out_shape=jax.Shape...]
where the time goes in v3:
time: 45.8 us; the launch traced here: 45.5 us
  Pallas kernels  40.7 us (89%)
  local copies, waits for them, and re-layouts  4.82 us (11%)
    pallas_call x1, Pallas kernels, dense_layer(): pl.pallas_call(functools.partial(dense_kernel, rows), out_shape=jax.Shape...  40.7 us
    unnamed x9, local copies, waits for them, and re-layouts  4.82 us

profile of v3, /device:TPU:0, one launch (start us, length us, event | category | flops | bytes accessed | tf_op | source)
XLA Modules:
  0.0 45.5 jit_solution(16785516336759071321)
XLA Ops:
  0.0 0.0 copy-start
  0.0 1.9 %copy-done = bf16[1,2048,768]{2,1,0:T(8,128)(2,1)S(1)} copy-done((bf16[1,2048,768]{2,1,0:T(8,128)(2,1)S(1)}, bf16[1,2048,768]{2,1,0:T(8,128)(2,1)}, u32[]{:S(2)}) %copy-start) | copy-done | bytes 3145752
  1.9 0.0 copy-start.1
  1.9 0.9 %copy-done.1 = bf16[128,512]{1,0:T(8,128)(2,1)S(1)} copy-done((bf16[128,512]{1,0:T(8,128)(2,1)S(1)}, bf16[128,512]{1,0:T(8,128)(2,1)}, u32[]{:S(2)}) %copy-start.1) | copy-done | bytes 131096
  2.8 0.0 copy-start.2
  2.8 0.7 %copy-done.2 = s32[128,8]{0,1:T(8,128)S(1)} copy-done((s32[128,8]{0,1:T(8,128)S(1)}, s32[128,8]{0,1:T(8,128)}, u32[]{:S(2)}) %copy-start.2) | copy-done | bytes 4120
  3.5 0.0 copy-start.3
  3.5 0.7 %copy-done.3 = f32[128,8]{0,1:T(8,128)S(1)} copy-done((f32[128,8]{0,1:T(8,128)S(1)}, f32[128,8]{0,1:T(8,128)}, u32[]{:S(2)}) %copy-start.3) | copy-done | bytes 4120
  4.2 40.7 %shard_map.64 = bf16[128,512]{1,0:T(8,128)(2,1)S(1)} custom-call(bf16[128,512]{1,0:T(8,128)(2,1)S(1)} %copy-done.1, s32[8,128]{1,0:T(8,128)S(1)} %bitcast.2, f32[8,128]{1,0:T(8,128)S(1)} %bitcast.3, bf16[1,2048,768]{2,1,0:T(8,128)(2,1)S(1)} %copy-done, bf16[1,2048,768]{2,1,0:T(8,128)(2,1)} %up_hbm.1, bf16[1,768,2048]{2,1,0:T(8,128)(2,1)} %down_hbm.1), custom_call_target="tpu_custom_call" | custom-call | flops 4831838208 | bytes 9437184 | tf_op jit(solution)/shard_map/pallas_call | solution.py:475
  44.9 0.7 %copy.8 = bf16[128,512]{1,0:T(8,128)(2,1)} copy(bf16[128,512]{1,0:T(8,128)(2,1)S(1)} %shard_map.64) | data formatting | bytes 262144
Async XLA Ops:
  0.0 1.9 %copy-start = (bf16[1,2048,768]{2,1,0:T(8,128)(2,1)S(1)}, bf16[1,2048,768]{2,1,0:T(8,128)(2,1)}, u32[]{:S(2)}) copy-start(bf16[1,2048,768]{2,1,0:T(8,128)(2,1)} %gate_hbm.1) | copy-start | bytes 9437188
  1.9 0.9 %copy-start.1 = (bf16[128,512]{1,0:T(8,128)(2,1)S(1)}, bf16[128,512]{1,0:T(8,128)(2,1)}, u32[]{:S(2)}) copy-start(bf16[128,512]{1,0:T(8,128)(2,1)} %acts_hbm.1) | copy-start | bytes 393220
  2.8 0.7 %copy-start.2 = (s32[128,8]{0,1:T(8,128)S(1)}, s32[128,8]{0,1:T(8,128)}, u32[]{:S(2)}) copy-start(s32[128,8]{0,1:T(8,128)} %param.7) | copy-start | bytes 12292
  3.5 0.7 %copy-start.3 = (f32[128,8]{0,1:T(8,128)S(1)}, f32[128,8]{0,1:T(8,128)}, u32[]{:S(2)}) copy-start(f32[128,8]{0,1:T(8,128)} %param.8) | copy-start | bytes 12292

commit v4 on v3

--- a/solution.py
+++ b/solution.py
@@ -288,13 +288,16 @@
         def _():
             gather_meta(r, side).start()
 
-    def cross(r):
+    def cross(r, q):
+        here = tokens(q)
+        given = kept[r, 1 - x, here] + core_in[r, 1 - x, here].astype(jnp.float32)
+        x_out[r, here] = given.astype(x_out.dtype)
+        reduce_x(r, q).start()
+
+    def begin_cross(r):
         reduce_core(r, 0).wait_recv()
         for q in range(CHUNKS):
-            here = tokens(q)
-            given = kept[r, 1 - x, here] + core_in[r, 1 - x, here].astype(jnp.float32)
-            x_out[r, here] = given.astype(x_out.dtype)
-            reduce_x(r, q).start()
+            cross(r, q)
         reduce_core(r, 1).wait_recv()
         total[r] = kept[r, x] + core_in[r, x].astype(jnp.float32)
 
@@ -365,7 +368,7 @@
 
             @pl.when(s == last)
             def _():
-                cross(z)
+                begin_cross(z)
 
         second_half(r)
 
@@ -380,41 +383,62 @@
     first_half(z)
     lax.fori_loop(0, rows, expert_step, 0)
 
-    if rows == 1:
-        cross(z)
-
-    def cross_step(t, carry):
-        cross(nth_row(last - t))
-        return carry
-
-    lax.fori_loop(0, last, cross_step, 0)
+    begin_cross(nth_row(last))
 
     def line_step(t, carry):
         r = nth_row(last - t)
+        following = nth_row(last - t - 1)
+        down, up = r < z, r > z
+        first = (down & (z == last)) | (up & (z == 0))
+
+        def send_on(q):
+            z_out[r, tokens(q)] = total[r, tokens(q)].astype(z_out.dtype)
+
+            @pl.when(down)
+            def _():
+                reduce_z(r, q, 0).start()
+
+            @pl.when(up)
+            def _():
+                reduce_z(r, q, 1).start()
+
+        @pl.when(t < last - 1)
+        def _():
+            reduce_core(following, 0).wait_recv()
+            reduce_core(following, 1).wait_recv()
+
         for q in range(CHUNKS):
             here = tokens(q)
             reduce_x(r, q).wait_recv()
+
+            @pl.when(t < last - 1)
+            def _():
+                cross(following, q)
+
             total[r, here] += x_in[r, here].astype(jnp.float32)
 
-            @pl.when((r < z) & (z < last))
+            @pl.when(first)
+            def _():
+                send_on(q)
+
+        @pl.when(t < last - 1)
+        def _():
+            total[following] = kept[following, x] + core_in[following, x].astype(jnp.float32)
+
+        for q in range(CHUNKS):
+            here = tokens(q)
+
+            @pl.when(down & (z < last))
             def _():
                 reduce_z(r, q, 0).wait_recv()
                 total[r, here] += z_in[0, r, here].astype(jnp.float32)
-
-            @pl.when((r > z) & (z > 0))
+                send_on(q)
+
+            @pl.when(up & (z > 0))
             def _():
                 reduce_z(r, q, 1).wait_recv()
                 total[r, here] += z_in[1, r, here].astype(jnp.float32)
-
-            z_out[r, here] = total[r, here].astype(z_out.dtype)
-
-            @pl.when(r < z)
-            def _():
-                reduce_z(r, q, 0).start()
-
-            @pl.when(r > z)
-            def _():
-                reduce_z(r, q, 1).start()
+                send_on(q)
 
         return carry
 
@@ -469,13 +493,13 @@
     top = expert_ids.shape[1]
     dtype = activations.dtype
     vmem = pl.BlockSpec(memory_space=pltpu.VMEM)
-    hbm = pl.BlockSpec(memory_space=pltpu.HBM)
+    anywhere = pl.BlockSpec(memory_space=pl.ANY)
     dma = pltpu.SemaphoreType.DMA
     flops = 6 * rows * group_rows * model * hidden
     return pl.pallas_call(
         functools.partial(dense_kernel, rows),
         out_shape=jax.ShapeDtypeStruct((group_rows, width), dtype),
-        in_specs=[hbm] * 6,
+        in_specs=[anywhere] * 6,
         out_specs=vmem,
         scratch_shapes=[
             pltpu.VMEM((rows, group_rows, model), dtype),
@@ -512,7 +536,7 @@
             dma((2, rows, CHUNKS)),
         ],
         compiler_params=pltpu.CompilerParams(
-            collective_id=0, has_side_effects=True, vmem_limit_bytes=48 * 1024 * 1024
+            collective_id=0, has_side_effects=True, vmem_limit_bytes=64 * 1024 * 1024
         ),
         cost_estimate=pl.CostEstimate(
             flops=flops, bytes_accessed=6 * model * hidden, transcendentals=rows * group_rows * hidden

time: 45.8 us -> 43.4 us (0.948)
  local copies, waits for them, and re-layouts: 4.82 us -> 1.57 us
  Pallas kernels: 40.7 us -> 41.7 us
    unnamed x9 -> x1, local copies, waits for them, and re-layouts: 4.82 us -> 1.57 us
    pallas_call x1, Pallas kernels: 40.7 us -> 41.7 us  [dense_layer(): pl.pallas_call(functools.partial(dense_kernel, rows), out_shape=jax.Shape...]
where the time goes in v4:
time: 43.4 us; the launch traced here: 43.2 us
  Pallas kernels  41.7 us (96%)
  local copies, waits for them, and re-layouts  1.57 us (4%)
    pallas_call x1, Pallas kernels, dense_layer(): pl.pallas_call(functools.partial(dense_kernel, rows), out_shape=jax.Shape...  41.7 us
    unnamed x1, local copies, waits for them, and re-layouts  1.57 us

profile of v4, /device:TPU:0, one launch (start us, length us, event | category | flops | bytes accessed | tf_op | source)
XLA Modules:
  0.0 43.2 jit_solution(12783430911776170249)
XLA Ops:
  0.0 41.7 %shard_map.64 = bf16[128,512]{1,0:T(8,128)(2,1)} custom-call(bf16[128,512]{1,0:T(8,128)(2,1)} %acts_hbm.1, s32[8,128]{1,0:T(8,128)} %bitcast.2, f32[8,128]{1,0:T(8,128)} %bitcast.3, bf16[1,2048,768]{2,1,0:T(8,128)(2,1)} %gate_hbm.1, bf16[1,2048,768]{2,1,0:T(8,128)(2,1)} %up_hbm.1, bf16[1,768,2048]{2,1,0:T(8,128)(2,1)} %down_hbm.1), custom_call_target="tpu_custom_call" | custom-call | flops 4831838208 | bytes 9437184 | tf_op jit(solution)/shard_map/pallas_call | solution.py:499
  41.7 1.6 %copy.8 = bf16[128,512]{1,0:T(8,128)(2,1)} copy(bf16[128,512]{1,0:T(8,128)(2,1)} %shard_map.64) | data formatting | bytes 262144

commit v5 on v4

--- a/solution.py
+++ b/solution.py
@@ -114,6 +114,8 @@
     x_in,
     z_out,
     z_in,
+    far_out,
+    far_in,
     weight_sem,
     own_sem,
     ag_z_send,
@@ -130,6 +132,10 @@
     rs_x_recv,
     rs_z_send,
     rs_z_recv,
+    ag_far_send,
+    ag_far_recv,
+    rs_far_send,
+    rs_far_recv,
 ):
     top, group_rows = ids_hbm.shape
     part = group_rows // CHUNKS
@@ -142,6 +148,15 @@
     across = {"col": (1 - x) * PAIR + core}
     last = rows - 1
 
+    far_chunk = CHUNKS - 1
+    ends = ((0, z < last, z > 0), (last, z > 0, z < last))
+
+    def at_end(r):
+        return (r == 0) | (r == last)
+
+    def by_x(r, q):
+        return jnp.logical_not(at_end(r)) | (r == z) if q == far_chunk else r >= 0
+
     def column(x_of, core_of):
         return pl.ds(pl.multiple_of((x_of * PAIR + core_of) * width, width), width)
 
@@ -219,6 +234,15 @@
             {"row": z + 2 * side - 1},
         )
 
+    def gather_far(i):
+        there = place(ends[i][0], far_chunk, 1 - x, core)
+        return remote(there, there, ag_far_send.at[i], ag_far_recv.at[i], {"row": z + 1 - 2 * i})
+
+    def reduce_far(i):
+        return remote(
+            far_out.at[i], far_in.at[i], rs_far_send.at[i], rs_far_recv.at[i], {"row": z + 2 * i - 1}
+        )
+
     weights = [
         pltpu.make_async_copy(src.at[0], dst, weight_sem.at[i])
         for i, (src, dst) in enumerate(((gate_hbm, gate_w), (up_hbm, up_w), (down_hbm, down_w)))
@@ -278,7 +302,10 @@
         def _():
             gather_z(r, q, side).start()
 
-        gather_x(r, q).start()
+        @pl.when(by_x(r, q))
+        def _():
+            gather_x(r, q).start()
+
         gather_core(r, q, 0).start()
 
     def pass_meta(r, side, more):
@@ -294,10 +321,14 @@
         x_out[r, here] = given.astype(x_out.dtype)
         reduce_x(r, q).start()
 
-    def begin_cross(r):
+    def begin_cross(r, skip):
         reduce_core(r, 0).wait_recv()
-        for q in range(CHUNKS):
-            cross(r, q)
+        for q in reversed(range(CHUNKS)):
+
+            @pl.when(jnp.logical_not(skip) if q == far_chunk else r >= 0)
+            def _():
+                cross(r, q)
+
         reduce_core(r, 1).wait_recv()
         total[r] = kept[r, x] + core_in[r, x].astype(jnp.float32)
 
@@ -357,8 +388,31 @@
 
         r = nth_row(s)
         for q in range(CHUNKS):
-            gather_x(r, q).wait_recv()
-            gather_core(r, q, 1, place(r, q, 1 - x, core)).start()
+
+            @pl.when(by_x(r, q))
+            def _():
+                gather_x(r, q).wait_recv()
+
+                if q == far_chunk:
+                    for i, (end, sends, _) in enumerate(ends):
+
+                        @pl.when((s == 0) & (z == end) & sends)
+                        def _():
+                            gather_far(i).start()
+
+                gather_core(r, q, 1, place(r, q, 1 - x, core)).start()
+
+        for i, (end, sends, _) in enumerate(ends):
+
+            @pl.when((s > 0) & ((z - s == end) if i == 0 else (z + s == end)))
+            def _():
+                gather_far(i).wait_recv()
+
+                @pl.when(sends)
+                def _():
+                    gather_far(i).start()
+
+                gather_core(end, far_chunk, 1, place(end, far_chunk, 1 - x, core)).start()
 
         @pl.when(s == 0)
         def _():
@@ -368,7 +422,7 @@
 
             @pl.when(s == last)
             def _():
-                begin_cross(z)
+                begin_cross(z, at_end(z))
 
         second_half(r)
 
@@ -383,13 +437,36 @@
     first_half(z)
     lax.fori_loop(0, rows, expert_step, 0)
 
-    begin_cross(nth_row(last))
+    furthest = nth_row(last)
+    begin_cross(furthest, furthest != z if rows > 1 else furthest < 0)
+
+    def drain_gather(r, carry):
+        for q in range(CHUNKS):
+
+            @pl.when(by_x(r, q))
+            def _():
+                gather_x(r, q).wait_send()
+
+            gather_core(r, q, 0).wait_send()
+            gather_core(r, q, 1).wait_send()
+
+        for side, sent in ((0, (r >= z) & (z > 0)), (1, (r <= z) & (z < last))):
+
+            @pl.when(sent)
+            def _():
+                gather_meta(r, side).wait_send()
+                for q in range(CHUNKS):
+                    gather_z(r, q, side).wait_send()
+
+        return carry
 
     def line_step(t, carry):
         r = nth_row(last - t)
         following = nth_row(last - t - 1)
         down, up = r < z, r > z
         first = (down & (z == last)) | (up & (z == 0))
+        is_end = at_end(r)
+        here_far = tokens(far_chunk)
 
         def send_on(q):
             z_out[r, tokens(q)] = total[r, tokens(q)].astype(z_out.dtype)
@@ -402,22 +479,42 @@
             def _():
                 reduce_z(r, q, 1).start()
 
+        def far_share():
+            return kept[r, 1 - x, here_far] + core_in[r, 1 - x, here_far].astype(jnp.float32)
+
+        for i, (end, _, _) in enumerate(ends):
+
+            @pl.when(first & (r == end))
+            def _():
+                far_out[i] = far_share().astype(far_out.dtype)
+                reduce_far(i).start()
+
+        @pl.when(first & is_end)
+        def _():
+            send_on(far_chunk)
+
         @pl.when(t < last - 1)
         def _():
             reduce_core(following, 0).wait_recv()
             reduce_core(following, 1).wait_recv()
 
-        for q in range(CHUNKS):
+        for q in reversed(range(CHUNKS)):
             here = tokens(q)
-            reduce_x(r, q).wait_recv()
-
-            @pl.when(t < last - 1)
+            crosses = by_x(r, q)
+
+            @pl.when(crosses)
+            def _():
+                reduce_x(r, q).wait_recv()
+
+            @pl.when((t < last - 1) & by_x(following, q))
             def _():
                 cross(following, q)
 
-            total[r, here] += x_in[r, here].astype(jnp.float32)
-
-            @pl.when(first)
+            @pl.when(crosses)
+            def _():
+                total[r, here] += x_in[r, here].astype(jnp.float32)
+
+            @pl.when(first & crosses)
             def _():
                 send_on(q)
 
@@ -425,7 +522,15 @@
         def _():
             total[following] = kept[following, x] + core_in[following, x].astype(jnp.float32)
 
-        for q in range(CHUNKS):
+        for i, (end, _, _) in enumerate(ends):
+
+            @pl.when((r == end) & jnp.logical_not(first))
+            def _():
+                reduce_far(i).wait_recv()
+                far_out[i] = (far_share() + far_in[i].astype(jnp.float32)).astype(far_out.dtype)
+                reduce_far(i).start()
+
+        for q in reversed(range(CHUNKS)):
             here = tokens(q)
 
             @pl.when(down & (z < last))
@@ -442,7 +547,26 @@
 
         return carry
 
+    lax.fori_loop(0, rows, drain_gather, 0)
+    for i, (_, sends, _) in enumerate(ends):
+
+        @pl.when(sends)
+        def _():
+            gather_far(i).wait_send()
+
     lax.fori_loop(0, last, line_step, 0)
+
+    if rows > 1:
+        here_far = tokens(far_chunk)
+        for i, (end, _, _) in enumerate(ends):
+
+            @pl.when(z == end)
+            def _():
+                reduce_far(i).wait_recv()
+                given = kept[z, 1 - x, here_far] + core_in[z, 1 - x, here_far].astype(jnp.float32)
+                x_out[z, here_far] = (given + far_in[i].astype(jnp.float32)).astype(x_out.dtype)
+                reduce_x(z, far_chunk).start()
+
     for q in range(CHUNKS):
         here = tokens(q)
         reduce_x(z, q).wait_recv()
@@ -464,26 +588,23 @@
         for which in range(2):
             reduce_core(r, which).wait_send()
         for q in range(CHUNKS):
-            gather_x(r, q).wait_send()
-            gather_core(r, q, 0).wait_send()
-            gather_core(r, q, 1).wait_send()
-            reduce_x(r, q).wait_send()
+
+            @pl.when(by_x(r, q))
+            def _():
+                reduce_x(r, q).wait_send()
 
             @pl.when(r != z)
             def _():
                 reduce_z(r, q, 0).wait_send()
 
-        for side, sent in ((0, (r >= z) & (z > 0)), (1, (r <= z) & (z < last))):
-
-            @pl.when(sent)
-            def _():
-                gather_meta(r, side).wait_send()
-                for q in range(CHUNKS):
-                    gather_z(r, q, side).wait_send()
-
         return carry
 
     lax.fori_loop(0, rows, drain, 0)
+    for i, (_, _, sends) in enumerate(ends):
+
+        @pl.when(sends)
+        def _():
+            reduce_far(i).wait_send()
 
 
 def dense_layer(activations, expert_ids, gate_scores, gate_proj, up_proj, down_proj):
@@ -518,6 +639,8 @@
             pltpu.VMEM((rows, group_rows, width), dtype),
             pltpu.VMEM((rows, group_rows, width), dtype),
             pltpu.VMEM((PAIR, rows, group_rows, width), dtype),
+            pltpu.VMEM((2, group_rows // CHUNKS, width), dtype),
+            pltpu.VMEM((2, group_rows // CHUNKS, width), dtype),
             dma((3,)),
             dma((3,)),
             dma((2, rows, CHUNKS)),
@@ -534,6 +657,10 @@
             dma((rows, CHUNKS)),
             dma((rows, CHUNKS)),
             dma((2, rows, CHUNKS)),
+            dma((2,)),
+            dma((2,)),
+            dma((2,)),
+            dma((2,)),
         ],
         compiler_params=pltpu.CompilerParams(
             collective_id=0, has_side_effects=True, vmem_limit_bytes=64 * 1024 * 1024

time: 43.4 us -> 42.2 us (0.972)
  Pallas kernels: 41.7 us -> 40.5 us
    pallas_call x1, Pallas kernels: 41.7 us -> 40.5 us  [dense_layer(): pl.pallas_call(functools.partial(dense_kernel, rows), out_shape=jax.Shape...]
where the time goes in v5:
time: 42.2 us; the launch traced here: 42.1 us
  Pallas kernels  40.5 us (96%)
  local copies, waits for them, and re-layouts  1.57 us (4%)
    pallas_call x1, Pallas kernels, dense_layer(): pl.pallas_call(functools.partial(dense_kernel, rows), out_shape=jax.Shape...  40.5 us
    unnamed x1, local copies, waits for them, and re-layouts  1.57 us

profile of v5, /device:TPU:0, one launch (start us, length us, event | category | flops | bytes accessed | tf_op | source)
XLA Modules:
  0.0 42.1 jit_solution(5175963602647723013)
XLA Ops:
  0.0 40.5 %shard_map.64 = bf16[128,512]{1,0:T(8,128)(2,1)} custom-call(bf16[128,512]{1,0:T(8,128)(2,1)} %acts_hbm.1, s32[8,128]{1,0:T(8,128)} %bitcast.2, f32[8,128]{1,0:T(8,128)} %bitcast.3, bf16[1,2048,768]{2,1,0:T(8,128)(2,1)} %gate_hbm.1, bf16[1,2048,768]{2,1,0:T(8,128)(2,1)} %up_hbm.1, bf16[1,768,2048]{2,1,0:T(8,128)(2,1)} %down_hbm.1), custom_call_target="tpu_custom_call" | custom-call | flops 4831838208 | bytes 9437184 | tf_op jit(solution)/shard_map/pallas_call | solution.py:620
  40.5 1.6 %copy.8 = bf16[128,512]{1,0:T(8,128)(2,1)} copy(bf16[128,512]{1,0:T(8,128)(2,1)} %shard_map.64) | data formatting | bytes 262144

commit v6 on v5

--- a/solution.py
+++ b/solution.py
@@ -9,7 +9,7 @@
 
 TOP = 8
 PAIR = 2
-CHUNKS = 2
+CHUNKS = 4
 MESH = pl.DeviceIdType.MESH
 
 

time: 42.2 us -> 42.1 us (level)
  no operation moved by 1% of the time
where the time goes in v6:
time: 42.1 us; the launch traced here: 41.7 us
  Pallas kernels  40.2 us (95%)
  local copies, waits for them, and re-layouts  1.57 us (4%)
    pallas_call x1, Pallas kernels, dense_layer(): pl.pallas_call(functools.partial(dense_kernel, rows), out_shape=jax.Shape...  40.2 us
    unnamed x1, local copies, waits for them, and re-layouts  1.57 us

profile of v6, /device:TPU:0, one launch (start us, length us, event | category | flops | bytes accessed | tf_op | source)
XLA Modules:
  0.0 41.7 jit_solution(12086888216339676111)
XLA Ops:
  0.0 40.2 %shard_map.64 = bf16[128,512]{1,0:T(8,128)(2,1)} custom-call(bf16[128,512]{1,0:T(8,128)(2,1)} %acts_hbm.1, s32[8,128]{1,0:T(8,128)} %bitcast.2, f32[8,128]{1,0:T(8,128)} %bitcast.3, bf16[1,2048,768]{2,1,0:T(8,128)(2,1)} %gate_hbm.1, bf16[1,2048,768]{2,1,0:T(8,128)(2,1)} %up_hbm.1, bf16[1,768,2048]{2,1,0:T(8,128)(2,1)} %down_hbm.1), custom_call_target="tpu_custom_call" | custom-call | flops 4831838208 | bytes 9437184 | tf_op jit(solution)/shard_map/pallas_call | solution.py:620
  40.2 1.6 %copy.8 = bf16[128,512]{1,0:T(8,128)(2,1)} copy(bf16[128,512]{1,0:T(8,128)(2,1)} %shard_map.64) | data formatting | bytes 262144

commit v7 on v5

--- a/solution.py
+++ b/solution.py
@@ -172,20 +172,28 @@
             src_ref=src, dst_ref=dst, send_sem=send, recv_sem=recv, device_id=device, device_id_type=MESH
         )
 
+    def position(r, at):
+        lower = at <= last - at
+        away = jnp.abs(r - at)
+        forward = jnp.where(lower, r > at, r < at)
+        both = 2 * away - jnp.where(forward, 1, 0)
+        return jnp.where(away <= jnp.minimum(at, last - at), both, jnp.where(lower, r, last - r))
+
     def tokens(q):
         return pl.ds(q * part, part)
 
-    def place(r, q, x_of, core_of):
-        return acts.at[r, tokens(q), column(x_of, core_of)]
+    def place(r, q, x_of, core_of, at=None):
+        slot = position(r, z if at is None else at)
+        return acts.at[slot, tokens(q), column(x_of, core_of)]
 
     def chunk_of(q):
         return acts_hbm.at[tokens(q)]
 
     def gather_z(r, q, side, src=None):
-        there = place(r, q, x, core)
+        to = jnp.clip(z + 2 * side - 1, 0, last)
         return remote(
-            there if src is None else src,
-            there,
+            place(r, q, x, core) if src is None else src,
+            place(r, q, x, core, to),
             ag_z_send.at[side, r, q],
             ag_z_recv.at[r, q],
             {"row": z + 2 * side - 1},
@@ -235,8 +243,9 @@
         )
 
     def gather_far(i):
-        there = place(ends[i][0], far_chunk, 1 - x, core)
-        return remote(there, there, ag_far_send.at[i], ag_far_recv.at[i], {"row": z + 1 - 2 * i})
+        end, to = ends[i][0], jnp.clip(z + 1 - 2 * i, 0, last)
+        here, there = place(end, far_chunk, 1 - x, core), place(end, far_chunk, 1 - x, core, to)
+        return remote(here, there, ag_far_send.at[i], ag_far_recv.at[i], {"row": z + 1 - 2 * i})
 
     def reduce_far(i):
         return remote(
@@ -248,7 +257,7 @@
         for i, (src, dst) in enumerate(((gate_hbm, gate_w), (up_hbm, up_w), (down_hbm, down_w)))
     ]
 
-    own = pltpu.make_async_copy(acts_hbm, acts.at[z, :, column(x, core)], own_sem.at[0])
+    own = pltpu.make_async_copy(acts_hbm, acts.at[0, :, column(x, core)], own_sem.at[0])
     own_ids = pltpu.make_async_copy(ids_hbm, ids, own_sem.at[1])
     own_scores = pltpu.make_async_copy(scores_hbm, meta.at[z, pl.ds(top, top)], own_sem.at[2])
     for copy in [own, own_ids, own_scores] + weights:
@@ -332,40 +341,49 @@
         reduce_core(r, 1).wait_recv()
         total[r] = kept[r, x] + core_in[r, x].astype(jnp.float32)
 
-    def product(r, x_of, core_of, table):
-        features = column(x_of, core_of)
-        return jnp.dot(acts[r, :, features], table[features, :], preferred_element_type=jnp.float32)
-
-    def first_half(r):
-        gate_sum[r] = product(r, x, core, gate_w)
-        up_sum[r] = product(r, x, core, up_w)
-        for q in range(CHUNKS):
-            gather_core(r, q, 0).wait_recv()
-        gate_sum[r] += product(r, x, 1 - core, gate_w)
-        up_sum[r] += product(r, x, 1 - core, up_w)
-
-    def second_half(r):
-        gate_sum[r] += product(r, 1 - x, core, gate_w)
-        up_sum[r] += product(r, 1 - x, core, up_w)
-        for q in range(CHUNKS):
-            gather_core(r, q, 1).wait_recv()
-        gate_val = gate_sum[r] + product(r, 1 - x, 1 - core, gate_w)
-        up_val = up_sum[r] + product(r, 1 - x, 1 - core, up_w)
+    batch = 2 if rows % 2 == 0 else 1
+    half = PAIR * width
+
+    def product(b, x_of, table):
+        features = pl.ds(pl.multiple_of(x_of * half, half), half)
+        block = acts[pl.ds(b * batch, batch), :, features].reshape(batch * group_rows, half)
+        return jnp.dot(block, table[features, :], preferred_element_type=jnp.float32)
+
+    def first_half(b):
+        for j in range(batch):
+            for q in range(CHUNKS):
+                gather_core(nth_row(b * batch + j), q, 0).wait_recv()
+        gate_sum[...] = product(b, x, gate_w)
+        up_sum[...] = product(b, x, up_w)
+
+    def second_half(b):
+        members = [nth_row(b * batch + j) for j in range(batch)]
+        for r in members:
+            for q in range(CHUNKS):
+                gather_core(r, q, 1).wait_recv()
+        gate_val = gate_sum[...] + product(b, 1 - x, gate_w)
+        up_val = up_sum[...] + product(b, 1 - x, up_w)
         hidden = (gate_val / (1.0 + jnp.exp(-gate_val)) * up_val).astype(jnp.bfloat16)
-        chosen = jnp.where(meta[r, :top] == expert.astype(jnp.float32), meta[r, top:], 0.0)
-        weight = jnp.sum(jnp.transpose(chosen), axis=1, keepdims=True)
+        scales = []
+        for r in members:
+            chosen = jnp.where(meta[r, :top] == expert.astype(jnp.float32), meta[r, top:], 0.0)
+            scales.append(jnp.sum(jnp.transpose(chosen), axis=1, keepdims=True))
 
         def weighted(x_of, core_of):
             result = jnp.dot(hidden, down_w[:, column(x_of, core_of)], preferred_element_type=jnp.float32)
-            return result * weight
+            result = result.reshape(batch, group_rows, width)
+            return [(r, result[j] * scales[j]) for j, r in enumerate(members)]
 
         for which, x_of in enumerate((1 - x, x)):
-            core_out[r, x_of] = weighted(x_of, 1 - core).astype(core_out.dtype)
-            reduce_core(r, which).start()
+            for r, result in weighted(x_of, 1 - core):
+                core_out[r, x_of] = result.astype(core_out.dtype)
+            for r in reversed(members):
+                reduce_core(r, which).start()
         for x_of in (1 - x, x):
-            kept[r, x_of] = weighted(x_of, core)
-
-    def expert_step(s, carry):
+            for r, result in weighted(x_of, core):
+                kept[r, x_of] = result
+
+    def arrivals(s):
         below, above = z - 1 - s, z + 1 + s
         from_below, from_above = below >= 0, above <= last
         for q in range(CHUNKS):
@@ -414,28 +432,30 @@
 
                 gather_core(end, far_chunk, 1, place(end, far_chunk, 1 - x, core)).start()
 
-        @pl.when(s == 0)
-        def _():
-            weights[2].wait()
-
-        if rows > 1:
-
-            @pl.when(s == last)
+    def expert_step(b, carry):
+        for j in range(batch):
+            arrivals(b * batch + j)
+            if j == max(0, batch - 2):
+
+                @pl.when(b == 0)
+                def _():
+                    for copy in weights:
+                        copy.wait()
+
+                first_half(b)
+        if rows > batch:
+
+            @pl.when(b == rows // batch - 1)
             def _():
                 begin_cross(z, at_end(z))
 
-        second_half(r)
-
-        @pl.when(s < last)
-        def _():
-            first_half(nth_row(s + 1))
-
+        second_half(b)
         return carry
 
-    for copy in weights[:2]:
-        copy.wait()
-    first_half(z)
-    lax.fori_loop(0, rows, expert_step, 0)
+    lax.fori_loop(0, rows // batch, expert_step, 0)
+
+    if rows == batch and rows > 1:
+        begin_cross(z, at_end(z))
 
     furthest = nth_row(last)
     begin_cross(furthest, furthest != z if rows > 1 else furthest < 0)
@@ -616,6 +636,7 @@
     vmem = pl.BlockSpec(memory_space=pltpu.VMEM)
     anywhere = pl.BlockSpec(memory_space=pl.ANY)
     dma = pltpu.SemaphoreType.DMA
+    batch = 2 if rows % 2 == 0 else 1
     flops = 6 * rows * group_rows * model * hidden
     return pl.pallas_call(
         functools.partial(dense_kernel, rows),
@@ -629,8 +650,8 @@
             pltpu.VMEM((model, hidden), dtype),
             pltpu.VMEM((model, hidden), dtype),
             pltpu.VMEM((hidden, model), dtype),
-            pltpu.VMEM((rows, group_rows, hidden), jnp.float32),
-            pltpu.VMEM((rows, group_rows, hidden), jnp.float32),
+            pltpu.VMEM((batch * group_rows, hidden), jnp.float32),
+            pltpu.VMEM((batch * group_rows, hidden), jnp.float32),
             pltpu.VMEM((rows, PAIR, group_rows, width), jnp.float32),
             pltpu.VMEM((rows, PAIR, group_rows, width), dtype),
             pltpu.VMEM((rows, PAIR, group_rows, width), dtype),

time: 42.2 us -> 41.9 us (level)
  no operation moved by 1% of the time
where the time goes in v7:
time: 41.9 us; the launch traced here: 41.8 us
  Pallas kernels  40.2 us (96%)
  local copies, waits for them, and re-layouts  1.57 us (4%)
    pallas_call x1, Pallas kernels, dense_layer(): pl.pallas_call(functools.partial(dense_kernel, rows), out_shape=jax.Shape...  40.2 us
    unnamed x1, local copies, waits for them, and re-layouts  1.57 us

profile of v7, /device:TPU:0, one launch (start us, length us, event | category | flops | bytes accessed | tf_op | source)
XLA Modules:
  0.0 41.8 jit_solution(14621756191595429058)
XLA Ops:
  0.0 40.2 %shard_map.64 = bf16[128,512]{1,0:T(8,128)(2,1)} custom-call(bf16[128,512]{1,0:T(8,128)(2,1)} %acts_hbm.1, s32[8,128]{1,0:T(8,128)} %bitcast.2, f32[8,128]{1,0:T(8,128)} %bitcast.3, bf16[1,2048,768]{2,1,0:T(8,128)(2,1)} %gate_hbm.1, bf16[1,2048,768]{2,1,0:T(8,128)(2,1)} %up_hbm.1, bf16[1,768,2048]{2,1,0:T(8,128)(2,1)} %down_hbm.1), custom_call_target="tpu_custom_call" | custom-call | flops 4831838208 | bytes 9437184 | tf_op jit(solution)/shard_map/pallas_call | solution.py:641
  40.2 1.6 %copy.8 = bf16[128,512]{1,0:T(8,128)(2,1)} copy(bf16[128,512]{1,0:T(8,128)(2,1)} %shard_map.64) | data formatting | bytes 262144

commit v8 on v7

--- a/solution.py
+++ b/solution.py
@@ -432,6 +432,9 @@
 
                 gather_core(end, far_chunk, 1, place(end, far_chunk, 1 - x, core)).start()
 
+    early = rows > batch
+    nearest = nth_row(min(1, last))
+
     def expert_step(b, carry):
         for j in range(batch):
             arrivals(b * batch + j)
@@ -443,22 +446,20 @@
                         copy.wait()
 
                 first_half(b)
-        if rows > batch:
-
-            @pl.when(b == rows // batch - 1)
-            def _():
-                begin_cross(z, at_end(z))
+                if early:
+
+                    @pl.when(b == rows // batch - 1)
+                    def _():
+                        begin_cross(z, at_end(z))
+                        begin_cross(nearest, at_end(nearest))
 
         second_half(b)
         return carry
 
     lax.fori_loop(0, rows // batch, expert_step, 0)
 
-    if rows == batch and rows > 1:
+    if not early and rows > 1:
         begin_cross(z, at_end(z))
-
-    furthest = nth_row(last)
-    begin_cross(furthest, furthest != z if rows > 1 else furthest < 0)
 
     def drain_gather(r, carry):
         for q in range(CHUNKS):
@@ -480,9 +481,7 @@
 
         return carry
 
-    def line_step(t, carry):
-        r = nth_row(last - t)
-        following = nth_row(last - t - 1)
+    def pass_line(r, following, more):
         down, up = r < z, r > z
         first = (down & (z == last)) | (up & (z == 0))
         is_end = at_end(r)
@@ -513,7 +512,7 @@
         def _():
             send_on(far_chunk)
 
-        @pl.when(t < last - 1)
+        @pl.when(more)
         def _():
             reduce_core(following, 0).wait_recv()
             reduce_core(following, 1).wait_recv()
@@ -526,7 +525,7 @@
             def _():
                 reduce_x(r, q).wait_recv()
 
-            @pl.when((t < last - 1) & by_x(following, q))
+            @pl.when(more & by_x(following, q))
             def _():
                 cross(following, q)
 
@@ -538,7 +537,7 @@
             def _():
                 send_on(q)
 
-        @pl.when(t < last - 1)
+        @pl.when(more)
         def _():
             total[following] = kept[following, x] + core_in[following, x].astype(jnp.float32)
 
@@ -565,8 +564,21 @@
                 total[r, here] += z_in[1, r, here].astype(jnp.float32)
                 send_on(q)
 
+    final = 1 if early else 0
+
+    def line_step(t, carry):
+        here = last - t
+        pass_line(nth_row(here), nth_row(here - 1), here - 1 > final)
         return carry
 
+    if early:
+
+        @pl.when(at_end(z))
+        def _():
+            pass_line(nearest, nearest, nearest < 0)
+
+    furthest = nth_row(last)
+    begin_cross(furthest, furthest != z if rows > 1 else furthest < 0)
     lax.fori_loop(0, rows, drain_gather, 0)
     for i, (_, sends, _) in enumerate(ends):
 
@@ -574,7 +586,12 @@
         def _():
             gather_far(i).wait_send()
 
-    lax.fori_loop(0, last, line_step, 0)
+    lax.fori_loop(0, last - final, line_step, 0)
+    if early:
+
+        @pl.when(jnp.logical_not(at_end(z)))
+        def _():
+            pass_line(nearest, nearest, nearest < 0)
 
     if rows > 1:
         here_far = tokens(far_chunk)

time: 41.9 us -> 44.5 us (1.062)
  Pallas kernels: 40.2 us -> 42.8 us
    pallas_call x1, Pallas kernels: 40.2 us -> 42.8 us  [dense_layer(): pl.pallas_call(functools.partial(dense_kernel, rows), out_shape=jax.Shape...]
where the time goes in v8:
time: 44.5 us; the launch traced here: 44.4 us
  Pallas kernels  42.8 us (96%)
  local copies, waits for them, and re-layouts  1.57 us (4%)
    pallas_call x1, Pallas kernels, dense_layer(): pl.pallas_call(functools.partial(dense_kernel, rows), out_shape=jax.Shape...  42.8 us
    unnamed x1, local copies, waits for them, and re-layouts  1.57 us

profile of v8, /device:TPU:0, one launch (start us, length us, event | category | flops | bytes accessed | tf_op | source)
XLA Modules:
  0.0 44.4 jit_solution(3500715872529087195)
XLA Ops:
  0.0 42.8 %shard_map.64 = bf16[128,512]{1,0:T(8,128)(2,1)} custom-call(bf16[128,512]{1,0:T(8,128)(2,1)} %acts_hbm.1, s32[8,128]{1,0:T(8,128)} %bitcast.2, f32[8,128]{1,0:T(8,128)} %bitcast.3, bf16[1,2048,768]{2,1,0:T(8,128)(2,1)} %gate_hbm.1, bf16[1,2048,768]{2,1,0:T(8,128)(2,1)} %up_hbm.1, bf16[1,768,2048]{2,1,0:T(8,128)(2,1)} %down_hbm.1), custom_call_target="tpu_custom_call" | custom-call | flops 4831838208 | bytes 9437184 | tf_op jit(solution)/shard_map/pallas_call | solution.py:658
  42.8 1.6 %copy.8 = bf16[128,512]{1,0:T(8,128)(2,1)} copy(bf16[128,512]{1,0:T(8,128)(2,1)} %shard_map.64) | data formatting | bytes 262144

commit v9 on v7

--- a/solution.py
+++ b/solution.py
@@ -260,7 +260,7 @@
     own = pltpu.make_async_copy(acts_hbm, acts.at[0, :, column(x, core)], own_sem.at[0])
     own_ids = pltpu.make_async_copy(ids_hbm, ids, own_sem.at[1])
     own_scores = pltpu.make_async_copy(scores_hbm, meta.at[z, pl.ds(top, top)], own_sem.at[2])
-    for copy in [own, own_ids, own_scores] + weights:
+    for copy in (own, own_ids, own_scores):
         copy.start()
 
     barrier = pltpu.get_barrier_semaphore()
@@ -290,6 +290,8 @@
 
     for q in range(CHUNKS):
         gather_core(z, q, 0, chunk_of(q)).start()
+    for copy in weights:
+        copy.start()
     own_ids.wait()
     own_scores.wait()
     meta[z, :top] = ids[...].astype(jnp.float32)
@@ -439,7 +441,7 @@
 
                 @pl.when(b == 0)
                 def _():
-                    for copy in weights:
+                    for copy in weights[:2]:
                         copy.wait()
 
                 first_half(b)
@@ -448,6 +450,10 @@
             @pl.when(b == rows // batch - 1)
             def _():
                 begin_cross(z, at_end(z))
+
+        @pl.when(b == 0)
+        def _():
+            weights[2].wait()
 
         second_half(b)
         return carry

time: 41.9 us -> 41.9 us (level)
  no operation moved by 1% of the time
where the time goes in v9:
time: 41.9 us; the launch traced here: 41.8 us
  Pallas kernels  40.2 us (96%)
  local copies, waits for them, and re-layouts  1.57 us (4%)
    pallas_call x1, Pallas kernels, dense_layer(): pl.pallas_call(functools.partial(dense_kernel, rows), out_shape=jax.Shape...  40.2 us
    unnamed x1, local copies, waits for them, and re-layouts  1.57 us

profile of v9, /device:TPU:0, one launch (start us, length us, event | category | flops | bytes accessed | tf_op | source)
XLA Modules:
  0.0 41.8 jit_solution(6939890135486195990)
XLA Ops:
  0.0 40.2 %shard_map.64 = bf16[128,512]{1,0:T(8,128)(2,1)} custom-call(bf16[128,512]{1,0:T(8,128)(2,1)} %acts_hbm.1, s32[8,128]{1,0:T(8,128)} %bitcast.2, f32[8,128]{1,0:T(8,128)} %bitcast.3, bf16[1,2048,768]{2,1,0:T(8,128)(2,1)} %gate_hbm.1, bf16[1,2048,768]{2,1,0:T(8,128)(2,1)} %up_hbm.1, bf16[1,768,2048]{2,1,0:T(8,128)(2,1)} %down_hbm.1), custom_call_target="tpu_custom_call" | custom-call | flops 4831838208 | bytes 9437184 | tf_op jit(solution)/shard_map/pallas_call | solution.py:647
  40.2 1.6 %copy.8 = bf16[128,512]{1,0:T(8,128)(2,1)} copy(bf16[128,512]{1,0:T(8,128)(2,1)} %shard_map.64) | data formatting | bytes 262144

commit v10 on v9

--- a/solution.py
+++ b/solution.py
@@ -466,6 +466,13 @@
     furthest = nth_row(last)
     begin_cross(furthest, furthest != z if rows > 1 else furthest < 0)
 
+    def cross_step(t, carry):
+        r = nth_row(last - t)
+        begin_cross(r, at_end(r))
+        return carry
+
+    lax.fori_loop(1, last, cross_step, 0)
+
     def drain_gather(r, carry):
         for q in range(CHUNKS):
 
@@ -488,7 +495,6 @@
 
     def line_step(t, carry):
         r = nth_row(last - t)
-        following = nth_row(last - t - 1)
         down, up = r < z, r > z
         first = (down & (z == last)) | (up & (z == 0))
         is_end = at_end(r)
@@ -519,11 +525,6 @@
         def _():
             send_on(far_chunk)
 
-        @pl.when(t < last - 1)
-        def _():
-            reduce_core(following, 0).wait_recv()
-            reduce_core(following, 1).wait_recv()
-
         for q in reversed(range(CHUNKS)):
             here = tokens(q)
             crosses = by_x(r, q)
@@ -532,10 +533,6 @@
             def _():
                 reduce_x(r, q).wait_recv()
 
-            @pl.when((t < last - 1) & by_x(following, q))
-            def _():
-                cross(following, q)
-
             @pl.when(crosses)
             def _():
                 total[r, here] += x_in[r, here].astype(jnp.float32)
@@ -543,10 +540,6 @@
             @pl.when(first & crosses)
             def _():
                 send_on(q)
-
-        @pl.when(t < last - 1)
-        def _():
-            total[following] = kept[following, x] + core_in[following, x].astype(jnp.float32)
 
         for i, (end, _, _) in enumerate(ends):
 

time: 41.9 us -> 42.2 us (level)
  no operation moved by 1% of the time
where the time goes in v10:
time: 42.2 us; the launch traced here: 42 us
  Pallas kernels  40.4 us (96%)
  local copies, waits for them, and re-layouts  1.57 us (4%)
    pallas_call x1, Pallas kernels, dense_layer(): pl.pallas_call(functools.partial(dense_kernel, rows), out_shape=jax.Shape...  40.4 us
    unnamed x1, local copies, waits for them, and re-layouts  1.57 us

profile of v10, /device:TPU:0, one launch (start us, length us, event | category | flops | bytes accessed | tf_op | source)
XLA Modules:
  0.0 42.0 jit_solution(9721968876413439402)
XLA Ops:
  0.0 40.4 %shard_map.64 = bf16[128,512]{1,0:T(8,128)(2,1)} custom-call(bf16[128,512]{1,0:T(8,128)(2,1)} %acts_hbm.1, s32[8,128]{1,0:T(8,128)} %bitcast.2, f32[8,128]{1,0:T(8,128)} %bitcast.3, bf16[1,2048,768]{2,1,0:T(8,128)(2,1)} %gate_hbm.1, bf16[1,2048,768]{2,1,0:T(8,128)(2,1)} %up_hbm.1, bf16[1,768,2048]{2,1,0:T(8,128)(2,1)} %down_hbm.1), custom_call_target="tpu_custom_call" | custom-call | flops 4831838208 | bytes 9437184 | tf_op jit(solution)/shard_map/pallas_call | solution.py:640
  40.5 1.6 %copy.8 = bf16[128,512]{1,0:T(8,128)(2,1)} copy(bf16[128,512]{1,0:T(8,128)(2,1)} %shard_map.64) | data formatting | bytes 262144
